TPU v7x, 128 devices: a whole 4x4x4 slice. The times are simulated.
128 devices in a mesh: replica: 4 (over y_lo, core), fsdp: 32 (over z, x, y_hi).
Axes of the slice: x: 4, y: 4 (y_hi: 2, y_lo: 2; y = y_hi * 2 + y_lo), z: 4, core: 2. Of those that a mesh axis runs over, the one named last changes fastest.
Arguments:
- inputs: bfloat16 [4, 4096, 4096], P('replica', 'fsdp'), may hold values from -6 to 6
- segments: int32 [4, 4096], P('replica', 'fsdp'), may hold values from 0 to 15, never falling along the last dimension, each value on 1 to 512 neighbouring positions
- cotangent: bfloat16 [4, 4096, 14336], P('replica', None, 'fsdp'), may hold values from -6 to 6
- base: float32 [4096, 14336], P('replica', 'fsdp'), may hold values from -6 to 6
- momentum: float32 [4096, 14336], P('replica', 'fsdp'), may hold values from -2 to 2
Outputs:
- new_base: float32 [4096, 14336], P('replica', 'fsdp')
- new_momentum: float32 [4096, 14336], P('replica', 'fsdp')
- weights: bfloat16 [4096, 14336], P(None, 'fsdp')
All inputs are finite; a program needn't handle non-finite values. Where the computation divides by a largest or mean magnitude, that divisor is 1e-20 or more.
Results may differ from a plain program's by a relative error of at most 0.0095.
Values may be sent and summed in bfloat16 or wider, within the bound.
A program may use at most 128 MiB of HBM per device.

v0:
```python
import jax
import jax.numpy as jnp
from jax import lax
from jax.sharding import PartitionSpec as P

D = 4096
BLOCK = 128
DOCS = 16


inner_rate = 2.0
outer_rate = 0.7
nesterov_coef = 0.9
epsilon = 1e-06


def body(inputs, segments, cotangent, base, momentum):
    local_cot = cotangent[0]
    columns = local_cot.shape[1]
    onehot = (segments[0][:, None] == jnp.arange(DOCS, dtype=jnp.int32)[None, :]).astype(
        jnp.float32
    )
    count = lax.psum(jnp.sum(onehot, axis=0), "fsdp")
    tok_weight = jnp.dot(onehot, 1.0 / count, precision=lax.Precision.HIGHEST)
    weighted = (inputs[0].astype(jnp.float32) * tok_weight[:, None]).astype(jnp.bfloat16)
    grad = lax.dot_general(
        lax.all_gather(weighted, "fsdp", axis=0, tiled=True),
        local_cot,
        (((0,), (0,)), ((), ())),
        preferred_element_type=jnp.float32,
    )
    outer = inner_rate * grad
    blocks = outer.reshape(D // BLOCK, BLOCK, columns)
    scale = (jnp.max(jnp.abs(blocks), axis=1) + epsilon).astype(jnp.bfloat16)
    coded = (blocks / scale[:, None, :].astype(jnp.float32)).astype(jnp.bfloat16)
    groups = lax.axis_size("replica")
    own_rows = D // groups
    decoded = (coded.astype(jnp.float32) * scale[:, None, :].astype(jnp.float32)).reshape(
        D, columns
    )
    summed = lax.psum(decoded, "replica")
    total = lax.dynamic_slice_in_dim(summed, lax.axis_index("replica") * own_rows, own_rows, 0)
    average = total / groups
    new_momentum = nesterov_coef * momentum + average
    new_base = base - outer_rate * (average + nesterov_coef * new_momentum)
    weights = lax.all_gather(new_base.astype(jnp.bfloat16), "replica", axis=0, tiled=True)
    return (new_base, new_momentum, weights)


def solution(mesh):
    return jax.shard_map(
        body,
        mesh=mesh,
        in_specs=(
            P("replica", "fsdp", None),
            P("replica", "fsdp"),
            P("replica", None, "fsdp"),
            P("replica", "fsdp"),
            P("replica", "fsdp"),
        ),
        out_specs=(P("replica", "fsdp"), P("replica", "fsdp"), P(None, "fsdp")),
        check_vma=False,
    )
```

profile of v0, /device:TPU:1, one launch (start us, length us, event | category | flops | bytes accessed | tf_op | source)
XLA Modules:
  0.0 619.3 jit_solution(278559645052686462)
XLA Ops:
  7.2 0.0 all-gather.3.cloned.1.call-start
  7.2 0.8 convert_reduce_fusion
  8.0 84.6 %psum.14 = f32[16]{0:T(128)S(1)} all-reduce(f32[16]{0:T(128)S(1)} %convert_reduce_fusion), channel_id=1, replica_groups=mesh['replica'=4,'fsdp'=32] {'fsdp'}, use_global_device_ids=true, to_apply=%region_1.0 | all-reduce | flops 16 | bytes 128 | tf_op jit(solution)/shard_map/psum | solution.py:23
  92.6 0.8 convolution_bitcast_fusion
  93.4 2.5 fusion.3
  95.8 0.0 all-gather.3.cloned.1.call-update
  95.8 0.0 all-reduce.2.cloned.1.call-start
  95.9 266.8 %all-gather.3.cloned.1.call-done = bf16[4096,4096]{1,0:T(8,128)(2,1)} async-done(((bf16[128,4096]{1,0:T(8,128)(2,1)}), bf16[4096,4096]{1,0:T(8,128)(2,1)}) %all-gather.3.cloned.1.call-update) | async-done | bytes 33554448 | tf_op jit(solution)/shard_map/all_gather | solution.py:27
  362.7 24.1 %fusion.1 = f32[4096,448]{0,1:T(8,128)} fusion(bf16[4096,4096]{1,0:T(8,128)(2,1)} %all-gather.3.cloned.1.call-done, bf16[1,4096,448]{1,2,0:T(8,128)(2,1)} %param.7), kind=kOutput, calls=%fused_computation.4 | convolution fusion | flops 15032385536 | bytes 44564480 | tf_op jit(solution)/shard_map/dot_general | solution.py:26
  386.8 4.6 abs_bitcast_fusion
  391.4 4.5 copy.8
  395.9 0.0 slice-start
  395.9 5.2 reduce_max.9
  401.1 0.0 slice-start.1
  401.2 4.2 div.21
  405.4 0.0 slice-done
  405.4 0.0 slice-done.1
  405.4 13.5 %bitcast_multiply_fusion = f32[4096,448]{0,1:T(8,128)} fusion(f32[56,8,32,128]{3,2,1,0:T(8,128)} %bitcast.31, f32[4096,448]{0,1:T(8,128)S(1)} %bitcast.30), kind=kLoop, calls=%fused_computation | loop fusion | flops 9175040 | bytes 22020096 | tf_op jit(solution)/shard_map/mul | solution.py:38
  418.9 0.0 copy-start
  418.9 0.0 all-reduce.2.cloned.1.call-update
  418.9 0.0 all-gather.5.cloned.1.call-start
  419.0 141.2 %all-reduce.2.cloned.1.call-done = f32[4096,448]{0,1:T(8,128)} async-done(((f32[4096,448]{0,1:T(8,128)}), f32[4096,448]{0,1:T(8,128)}) %all-reduce.2.cloned.1.call-update) | async-done | bytes 7340048 | tf_op jit(solution)/shard_map/psum | solution.py:41
  560.2 0.0 copy-done
  560.2 5.1 fusion.8
  565.3 0.0 all-gather.5.cloned.1.call-update
  565.3 43.2 %all-gather.5.cloned.1.call-done = bf16[4096,448]{0,1:T(8,128)(2,1)} async-done(((bf16[1024,448]{0,1:T(8,128)(2,1)}), bf16[4096,448]{0,1:T(8,128)(2,1)}) %all-gather.5.cloned.1.call-update) | async-done | bytes 3670032 | tf_op jit(solution)/shard_map/all_gather | solution.py:46
  608.5 4.3 copy.16
  (2 shorter events, 0.0 us)
Async XLA Ops:
  7.2 355.6 %all-gather.3.cloned.1.call-start = ((), (), s32[]{:S(2)}) async-start(), calls=%async_computation | async-start | bytes 34603008 | tf_op jit(solution)/shard_map/all_gather | solution.py:27
  95.8 464.3 %all-reduce.2.cloned.1.call-start = ((), (), s32[]{:S(2)}) async-start(), calls=%async_computation.1 | async-start | bytes 14680064 | tf_op jit(solution)/shard_map/psum | solution.py:41
  395.9 9.5 %slice-start = ((s8[7340032]{0:T(1024)(128)(4,1)}), s8[3145728]{0:T(1024)(128)(4,1)S(1)}, s32[]{:S(2)}) async-start(s8[7340032]{0:T(1024)(128)(4,1)} %bitcast.29), calls=%async_computation.3 | async-start | bytes 6291456
  401.1 4.3 slice-start.1
  418.9 141.3 %copy-start = (f32[1024,448]{0,1:T(8,128)S(1)}, f32[1024,448]{0,1:T(8,128)}, u32[]{:S(2)}) copy-start(f32[1024,448]{0,1:T(8,128)} %param.8) | copy-start | bytes 5505028
  418.9 189.6 %all-gather.5.cloned.1.call-start = ((), (), s32[]{:S(2)}) async-start(), calls=%async_computation.2 | async-start | bytes 4587520 | tf_op jit(solution)/shard_map/all_gather | solution.py:46
Sparse Core Ops, SparseCore 0:
  96.0 266.7 all-gather.2
  419.0 141.0 all-reduce.1
  565.4 43.0 all-gather.4
where the time goes:
time: 620 us; the launch traced here: 619 us
  waiting for transfers between devices  451 us (73%)
  blocking collectives  84.6 us (14%)
  other arithmetic  31.7 us (5%)
  matrix products  24.8 us (4%)
  between operations  13.8 us (2%)
  local copies, waits for them, and re-layouts  13 us (2%)
    all_gather x1, waiting for transfers between devices, body(): lax.all_gather(weighted, 'fsdp', axis=0, tiled=True)  267 us
    psum x1, waiting for transfers between devices, body(): summed = lax.psum(decoded, 'replica')  141 us
    psum x1, blocking collectives, body(): count = lax.psum(jnp.sum(onehot, axis=0), 'fsdp')  84.6 us
    all_gather x1, waiting for transfers between devices, body(): lax.all_gather(new_base.astype(jnp.bfloat16), 'replica', axis=0, tiled=True)  43.2 us
    dot_general x1, matrix products, body(): lax.dot_general(lax.all_gather(weighted, 'fsdp', axis=0, tiled=True), loc...  24.1 us
    mul x1, other arithmetic, body(): coded.astype(jnp.float32) * scale[:, None, :].astype(jnp.float32)  13.5 us
  transfers between devices with their start and end apart: 3, of which 3 were waited for; matrix products, arithmetic and copies ran while one was open for 0% of the time, Pallas kernels for 0%

commit v1 on v0

v1 whole, which is shorter than its diff:
```python
import jax
import jax.numpy as jnp
from jax import lax
from jax.experimental import pallas as pl
from jax.experimental.pallas import tpu as pltpu
from jax.sharding import PartitionSpec as P

D = 4096
BLOCK = 128
DOCS = 16
STEPS = 8
SIDE = 4
TOK = 128
COLS = 448
HALF = D // 2
OWN = D // 4
EARLY = 3

inner_rate = 2.0
outer_rate = 0.7
nesterov_coef = 0.9
epsilon = 1e-06
MESH = pl.DeviceIdType.MESH


def kernel(
    seg_ref, inp_ref, cot_ref, base_ref, mom_ref,
    nb_out, nm_out, w_out,
    xin, xa, xb, ysend, cot, base, mom, acc, keep, xs, xr, ps, rr, wt, cnt,
    load_sem, cot_sem, cnt_send, cnt_recv,
    a1s, a1r, a2s, a2r, b1s, b1r, b2s, b2r, ys, yr, cots, cotr,
    xss, xsr, pss, psr, wcs, wcr, wls, wlr, wfs, wfr, out_sem,
):
    rep, f = lax.axis_index("replica"), lax.axis_index("fsdp")
    lo, core = rep // 2, rep % 2
    z, x, h = f // 8, (f // 2) % 4, f % 2

    def dev(x_=x, z_=z, h_=h, lo_=lo, core_=core):
        return (lo_ * 2 + core_, z_ * 8 + x_ * 2 + h_)

    def rot(v, d):
        return lax.rem(v + d, SIDE)

    other_core = dev(core_=1 - core)
    other_lo = dev(lo_=1 - lo)
    other_h = dev(h_=1 - h)

    def remote(src, dst, ss, rs, to):
        return pltpu.make_async_remote_copy(
            src_ref=src, dst_ref=dst, send_sem=ss, recv_sem=rs, device_id=to, device_id_type=MESH
        )

    load_in = pltpu.make_async_copy(inp_ref, xin, load_sem.at[0])
    load_base = pltpu.make_async_copy(base_ref, base, load_sem.at[1])
    load_mom = pltpu.make_async_copy(mom_ref, mom, load_sem.at[2])
    load_in.start()

    barrier = pltpu.get_barrier_semaphore()
    partners = [dev(x_=rot(x, d)) for d in (1, 2, 3)] + [dev(z_=rot(z, d)) for d in (1, 2, 3)]
    partners += [other_core, other_lo, other_h, dev(h_=1 - h, lo_=1 - lo)]
    for to in partners:
        pl.semaphore_signal(barrier, inc=1, device_id=to, device_id_type=MESH)
    pl.semaphore_wait(barrier, len(partners))

    def cot_rows(zz, xx, hh):
        return cot_ref.at[pl.ds(pl.multiple_of((zz * 8 + xx * 2 + hh) * TOK, TOK), TOK)]

    def send_cot(i, carry):
        zz, xx = i // 4, i % 4
        remote(cot_rows(zz, xx, 1 - h), cot.at[1, 0, zz, xx], cots, cotr, other_h).start()
        remote(cot_rows(zz, xx, h), cot.at[1, 1, xx, zz], cots, cotr, other_h).start()
        return carry

    def load_cot(i, carry):
        zz, xx = i // 4, i % 4
        pltpu.make_async_copy(cot_rows(zz, xx, h), cot.at[0, 0, zz, xx], cot_sem).start()
        pltpu.make_async_copy(cot_rows(zz, xx, 1 - h), cot.at[0, 1, xx, zz], cot_sem).start()
        return carry

    onehot = (seg_ref[...] == lax.broadcasted_iota(jnp.int32, (DOCS, TOK), 0)).astype(jnp.float32)
    count = jnp.broadcast_to(jnp.sum(onehot, axis=1, keepdims=True), (DOCS, TOK))
    for phase, (own, size) in enumerate(((x, SIDE), (z, SIDE), (h, 2))):
        cnt[phase, 0] = count
        for d in range(1, size):
            to = (dev(x_=rot(x, d)), dev(z_=rot(z, d)), other_h)[phase]
            remote(cnt.at[phase, 0], cnt.at[phase, d], cnt_send.at[phase, d], cnt_recv.at[phase, d], to).start()
        if phase == 0:
            lax.fori_loop(0, EARLY, send_cot, 0)
        for d in range(1, size):
            to = (dev(x_=rot(x, d)), dev(z_=rot(z, d)), other_h)[phase]
            remote(cnt.at[phase, 0], cnt.at[phase, d], cnt_send.at[phase, d], cnt_recv.at[phase, d], to).wait()
            count = count + cnt[phase, d]
    tok_row = jnp.sum(onehot * (1.0 / count), axis=0, keepdims=True)
    tok_weight = jnp.transpose(jnp.broadcast_to(tok_row, (TOK, TOK)))

    load_in.wait()

    def a1(s, d):
        return remote(xa.at[s, z, x], xa.at[s, z, x], a1s.at[s, d], a1r.at[s, d], dev(x_=rot(x, d + 1)))

    def a2(s, d):
        return remote(xa.at[s, z], xa.at[s, z], a2s.at[s, d], a2r.at[s, d], dev(z_=rot(z, d + 1)))

    def b1(s, d):
        return remote(xb.at[s, x, z], xb.at[s, x, z], b1s.at[s, d], b1r.at[s, d], dev(z_=rot(z, d + 1)))

    def b2(s, d):
        return remote(xb.at[s, x], xb.at[s, x], b2s.at[s, d], b2r.at[s, d], dev(x_=rot(x, d + 1)))

    def cross(s):
        return remote(ysend.at[s], xb.at[s, x, z], ys.at[s], yr.at[s], other_h)

    def weigh(s, carry):
        for part in (0, 1):
            for half in (0, 1):
                hh = h if half == 0 else 1 - h
                at = pl.multiple_of(hh * HALF + part * OWN + s * BLOCK, BLOCK)
                w = (xin[:, pl.ds(at, BLOCK)].astype(jnp.float32) * tok_weight).astype(jnp.bfloat16)
                if half == 0:
                    xa[s, z, x, :, part * BLOCK : (part + 1) * BLOCK] = w
                else:
                    ysend[s, :, part * BLOCK : (part + 1) * BLOCK] = w
        cross(s).start()
        for d in range(3):
            a1(s, d).start()
        return carry

    lax.fori_loop(0, STEPS, weigh, 0)
    lax.fori_loop(0, 16, load_cot, 0)
    load_base.start()
    load_mom.start()

    def relay(s, carry):
        @pl.when(s < STEPS)
        def _():
            for d in range(3):
                a1(s, d).wait_recv()
            for d in range(3):
                a2(s, d).start()
            cross(s).wait_recv()
            for d in range(3):
                b1(s, d).start()

        @pl.when(s >= 1)
        def _():
            for d in range(3):
                b1(s - 1, d).wait_recv()
            for d in range(3):
                b2(s - 1, d).start()

        return carry

    lax.fori_loop(EARLY, 16, send_cot, 0)
    lax.fori_loop(0, STEPS + 1, relay, 0)
    pltpu.make_async_copy(cot.at[0], cot.at[0], cot_sem).wait()

    def swap(j):
        return remote(xs.at[j], xr.at[j], xss.at[j], xsr.at[j], other_core)

    def to_owner(j, s, w):
        c = jnp.where(w == 0, h, 1 - h)
        return remote(ps.at[j], rr.at[s, lo], pss.at[j], psr.at[s, lo], dev(h_=c, lo_=h))

    def from_owner(s, src):
        return remote(ps.at[0], rr.at[s, src], pss.at[0], psr.at[s, src], other_lo)

    def rows(rp, s):
        return pl.ds(pl.multiple_of(rp * OWN + s * BLOCK, BLOCK), BLOCK)

    def w_core(s):
        return remote(wt.at[s], w_out.at[rows(rep, s)], wcs.at[s], wcr.at[s], other_core)

    def w_lo(s):
        return remote(wt.at[s], w_out.at[rows(rep, s)], wls.at[s], wlr.at[s], other_lo)

    def w_fwd(s):
        there = rows((1 - lo) * 2 + core, s)
        return remote(w_out.at[there], w_out.at[there], wfs.at[s], wfr.at[s], other_core)

    def quantized(at):
        blk = inner_rate * acc[pl.ds(pl.multiple_of(at * BLOCK, BLOCK), BLOCK), :]
        scale = (jnp.max(jnp.abs(blk), axis=0, keepdims=True) + epsilon).astype(jnp.bfloat16)
        scale = scale.astype(jnp.float32)
        coded = (blk * (1.0 / scale)).astype(jnp.bfloat16)
        return coded.astype(jnp.float32) * scale

    def step(j, carry):
        @pl.when(j < 2 * STEPS)
        def _():
            w, s = j // STEPS, j % STEPS

            @pl.when(j < STEPS)
            def _():
                for d in range(3):
                    a2(s, d).wait_recv()
                    b2(s, d).wait_recv()

            @pl.when(j == STEPS)
            def _():
                pltpu.make_async_copy(cot.at[1], cot.at[1], cotr).wait()

            acc[...] = jnp.zeros_like(acc)

            def part_a(k, c):
                acc[...] += lax.dot_general(
                    xa[s, k].reshape(SIDE * TOK, 2 * BLOCK), cot[w, 0, k].reshape(SIDE * TOK, COLS),
                    (((0,), (0,)), ((), ())), preferred_element_type=jnp.float32,
                )
                acc[...] += lax.dot_general(
                    xb[s, k].reshape(SIDE * TOK, 2 * BLOCK), cot[w, 1, k].reshape(SIDE * TOK, COLS),
                    (((0,), (0,)), ((), ())), preferred_element_type=jnp.float32,
                )
                return c

            lax.fori_loop(0, SIDE, part_a, 0)
            xs[j] = quantized(1 - core)
            swap(j).start()

        @pl.when((j >= 1) & (j <= 2 * STEPS))
        def _():
            q = j - 1
            w, s = q // STEPS, q % STEPS
            swap(q).wait_recv()
            ps[q] = (keep[...] + xr[q]).astype(jnp.bfloat16)
            local = (w == 0) & (lo == h)

            @pl.when(local)
            def _():
                rr[s, lo] = ps[q]

            @pl.when(jnp.logical_not(local))
            def _():
                to_owner(q, s, w).start()

        @pl.when(j < 2 * STEPS)
        def _():
            keep[...] = quantized(core)

        @pl.when(j == STEPS)
        def _():
            load_base.wait()
            load_mom.wait()

        @pl.when((j >= STEPS + 3) & (j < 2 * STEPS + 3))
        def _():
            s = j - (STEPS + 3)
            from_owner(s, 1 - lo).wait_recv()

            @pl.when(lo != h)
            def _():
                from_owner(s, lo).wait_recv()

            average = (rr[s, 0].astype(jnp.float32) + rr[s, 1].astype(jnp.float32)) * 0.25
            at = pl.ds(pl.multiple_of(s * BLOCK, BLOCK), BLOCK)
            nm = nesterov_coef * mom[at, :] + average
            nb = base[at, :] - outer_rate * (average + nesterov_coef * nm)
            mom[at, :] = nm
            base[at, :] = nb
            wt[s] = nb.astype(jnp.bfloat16)
            w_lo(s).start()
            w_core(s).start()
            pltpu.make_async_copy(wt.at[s], w_out.at[rows(rep, s)], out_sem.at[0, s]).start()
            pltpu.make_async_copy(mom.at[at], nm_out.at[at], out_sem.at[1, s]).start()
            pltpu.make_async_copy(base.at[at], nb_out.at[at], out_sem.at[2, s]).start()

        @pl.when(j >= STEPS + 5)
        def _():
            s = j - (STEPS + 5)
            w_lo(s).wait_recv()
            w_fwd(s).start()

        return carry

    lax.fori_loop(0, 2 * STEPS + 5, step, 0)

    def finish(s, carry):
        for d in range(3):
            a1(s, d).wait_send()
            a2(s, d).wait_send()
            b1(s, d).wait_send()
            b2(s, d).wait_send()
        cross(s).wait_send()
        swap(s).wait_send()
        swap(s + STEPS).wait_send()

        @pl.when(lo != h)
        def _():
            to_owner(s, s, 0).wait_send()

        to_owner(s + STEPS, s, 1).wait_send()
        w_core(s).wait_send()
        w_lo(s).wait_send()
        w_fwd(s).wait_send()
        w_core(s).wait_recv()
        w_fwd(s).wait_recv()
        at = pl.ds(pl.multiple_of(s * BLOCK, BLOCK), BLOCK)
        pltpu.make_async_copy(wt.at[s], w_out.at[rows(rep, s)], out_sem.at[0, s]).wait()
        pltpu.make_async_copy(mom.at[at], nm_out.at[at], out_sem.at[1, s]).wait()
        pltpu.make_async_copy(base.at[at], nb_out.at[at], out_sem.at[2, s]).wait()
        return carry

    lax.fori_loop(0, STEPS, finish, 0)
    pltpu.make_async_copy(cot.at[1], cot.at[1], cots).wait()


def body(inputs, segments, cotangent, base, momentum):
    bf, f32, dma = jnp.bfloat16, jnp.float32, pltpu.SemaphoreType.DMA
    hbm = pl.BlockSpec(memory_space=pl.ANY)
    return pl.pallas_call(
        kernel,
        out_shape=(
            jax.ShapeDtypeStruct((OWN, COLS), f32),
            jax.ShapeDtypeStruct((OWN, COLS), f32),
            jax.ShapeDtypeStruct((D, COLS), bf),
        ),
        in_specs=[pl.BlockSpec(memory_space=pltpu.VMEM), hbm, hbm, hbm, hbm],
        out_specs=(hbm, hbm, hbm),
        scratch_shapes=[
            pltpu.VMEM((TOK, D), bf),
            pltpu.VMEM((STEPS, SIDE, SIDE, TOK, 2 * BLOCK), bf),
            pltpu.VMEM((STEPS, SIDE, SIDE, TOK, 2 * BLOCK), bf),
            pltpu.VMEM((STEPS, TOK, 2 * BLOCK), bf),
            pltpu.VMEM((2, 2, SIDE, SIDE, TOK, COLS), bf),
            pltpu.VMEM((OWN, COLS), f32),
            pltpu.VMEM((OWN, COLS), f32),
            pltpu.VMEM((2 * BLOCK, COLS), f32),
            pltpu.VMEM((BLOCK, COLS), f32),
            pltpu.VMEM((2 * STEPS, BLOCK, COLS), f32),
            pltpu.VMEM((2 * STEPS, BLOCK, COLS), f32),
            pltpu.VMEM((2 * STEPS, BLOCK, COLS), bf),
            pltpu.VMEM((STEPS, 2, BLOCK, COLS), bf),
            pltpu.VMEM((STEPS, BLOCK, COLS), bf),
            pltpu.VMEM((3, SIDE, DOCS, TOK), f32),
            dma((3,)), dma, dma((3, SIDE)), dma((3, SIDE)),
            dma((STEPS, 3)), dma((STEPS, 3)), dma((STEPS, 3)), dma((STEPS, 3)),
            dma((STEPS, 3)), dma((STEPS, 3)), dma((STEPS, 3)), dma((STEPS, 3)),
            dma((STEPS,)), dma((STEPS,)), dma, dma,
            dma((2 * STEPS,)), dma((2 * STEPS,)), dma((2 * STEPS,)), dma((STEPS, 2)),
            dma((STEPS,)), dma((STEPS,)), dma((STEPS,)), dma((STEPS,)),
            dma((STEPS,)), dma((STEPS,)), dma((3, STEPS)),
        ],
        compiler_params=pltpu.CompilerParams(
            collective_id=0, has_side_effects=True, vmem_limit_bytes=60 * 2**20
        ),
        cost_estimate=pl.CostEstimate(flops=2 * D * D * COLS, bytes_accessed=2**24, transcendentals=0),
    )(segments, inputs[0], cotangent[0], base, momentum)


def solution(mesh):
    return jax.shard_map(
        body,
        mesh=mesh,
        in_specs=(
            P("replica", "fsdp", None),
            P("replica", "fsdp"),
            P("replica", None, "fsdp"),
            P("replica", "fsdp"),
            P("replica", "fsdp"),
        ),
        out_specs=(P("replica", "fsdp"), P("replica", "fsdp"), P(None, "fsdp")),
        check_vma=False,
    )
```

time: 620 us -> 247 us (0.40)
  waiting for transfers between devices: 451 us -> 0 us
  Pallas kernels: 0 us -> 223 us
  blocking collectives: 84.6 us -> 0 us
  other arithmetic: 31.7 us -> 0 us
  matrix products: 24.8 us -> 0 us
  between operations: 13.8 us -> 0.66 us
  local copies, waits for them, and re-layouts: 13 us -> 22.2 us
    all_gather x2 -> x0, waiting for transfers between devices: 310 us -> none  [the longest x1 267 us: body(): lax.all_gather(weighted, 'fsdp', axis=0, tiled=True)]
    pallas_call x0 -> x1, Pallas kernels: none -> 223 us  [body(): pl.pallas_call(kernel, out_shape=(jax.ShapeDtypeStruct((OWN, COLS), f32),...]
    psum x1 -> x0, waiting for transfers between devices: 141 us -> none  [body(): summed = lax.psum(decoded, 'replica')]
    psum x1 -> x0, blocking collectives: 84.6 us -> none  [body(): count = lax.psum(jnp.sum(onehot, axis=0), 'fsdp')]
    dot_general x2 -> x0, matrix products: 24.8 us -> none  [the longest x1 24.1 us: body(): lax.dot_general(lax.all_gather(weighted, 'fsdp', axis=0, tiled=True), loc...]
    mul x1 -> x0, other arithmetic: 13.5 us -> none  [body(): coded.astype(jnp.float32) * scale[:, None, :].astype(jnp.float32)]
    pallas_call x0 -> x3, local copies, waits for them, and re-layouts: none -> 10.9 us  [body(): pl.pallas_call(kernel, out_shape=(jax.ShapeDtypeStruct((OWN, COLS), f32),...]
    convert_element_type x3 -> x0, other arithmetic: 7.58 us -> none  [the longest x1 5.1 us: body(): new_base.astype(jnp.bfloat16)]
  transfers between devices with their start and end apart: 3 -> 0, of which waited for: 3 -> 0; matrix products, arithmetic and copies ran while one was open for 0% -> 0% of each run, Pallas kernels for 0% -> 0%
where the time goes in v1:
time: 247 us; the launch traced here: 246 us
  Pallas kernels  223 us (90%)
  local copies, waits for them, and re-layouts  22.2 us (9%)
    pallas_call x1, Pallas kernels, body(): pl.pallas_call(kernel, out_shape=(jax.ShapeDtypeStruct((OWN, COLS), f32),...  223 us
    unnamed x7, local copies, waits for them, and re-layouts  11.3 us
    pallas_call x3, local copies, waits for them, and re-layouts, body(): pl.pallas_call(kernel, out_shape=(jax.ShapeDtypeStruct((OWN, COLS), f32),...  10.9 us

profile of v1, /device:TPU:1, one launch (start us, length us, event | category | flops | bytes accessed | tf_op | source)
XLA Modules:
  0.0 246.2 jit_solution(11718602120747039975)
XLA Ops:
  0.6 0.0 copy-start.1
  0.6 3.0 %copy.9.base_ref = f32[1024,448]{1,0:T(8,128)} copy(f32[1024,448]{0,1:T(8,128)} %param.8) | data formatting | bytes 3670016 | tf_op args[3]
  3.6 0.0 copy-done.1
  3.6 1.8 copy.10.mom_ref
  5.5 6.4 %copy.8 = bf16[1,4096,448]{2,1,0:T(8,128)(2,1)} copy(bf16[1,4096,448]{1,2,0:T(8,128)(2,1)} %param.7) | data formatting | bytes 7340032 | tf_op args[2]
  11.9 223.4 %shard_map.76 = (f32[1024,448]{1,0:T(8,128)}, f32[1024,448]{1,0:T(8,128)}, bf16[4096,448]{1,0:T(8,128)(2,1)}) custom-call(s32[1,128]{1,0:T(1,128)} %seg_ref.1, bf16[128,4096]{1,0:T(8,128)(2,1)} %bitcast.3, bf16[4096,448]{1,0:T(8,128)(2,1)} %bitcast.2, f32[1024,448]{1,0:T(8,128)} %copy.9.base_ref, f32[1024,448]{1,0:T(8,128)} %copy.10.mom_ref), custom_call_target="tpu_custom_call" | custom-call | flops 15032385536 | bytes 16777216 | tf_op jit(solution)/shard_map/pallas_call | solution.py:309
  235.3 0.0 copy-start
  235.3 2.9 %copy.11 = f32[1024,448]{0,1:T(8,128)} copy(f32[1024,448]{1,0:T(8,128)} %get-tuple-element.3) | data formatting | bytes 3670016 | tf_op jit(solution)/shard_map/pallas_call | solution.py:309
  238.2 0.0 copy-done
  238.2 1.7 copy.12
  240.0 6.3 %copy.13 = bf16[4096,448]{0,1:T(8,128)(2,1)} copy(bf16[4096,448]{1,0:T(8,128)(2,1)} %get-tuple-element.5) | data formatting | bytes 7340032 | tf_op jit(solution)/shard_map/pallas_call | solution.py:309
Async XLA Ops:
  0.6 3.0 %copy-start.1 = (f32[1024,448]{0,1:T(8,128)S(1)}, f32[1024,448]{0,1:T(8,128)}, u32[]{:S(2)}) copy-start(f32[1024,448]{0,1:T(8,128)} %param.9) | copy-start | bytes 5505028
  235.3 3.0 %copy-start = (f32[1024,448]{1,0:T(8,128)S(1)}, f32[1024,448]{1,0:T(8,128)}, u32[]{:S(2)}) copy-start(f32[1024,448]{1,0:T(8,128)} %get-tuple-element.4) | copy-start | bytes 5505028

commit v2 on v0

v2 whole, which is shorter than its diff:
```python
import jax
import jax.numpy as jnp
from jax import lax
from jax.experimental import pallas as pl
from jax.experimental.pallas import tpu as pltpu
from jax.sharding import PartitionSpec as P

D = 4096
BLOCK = 128
DOCS = 16
STEPS = 8
SIDE = 4
TOK = 128
TOK_G = 4096
COLS = 448
HALF = D // 2
OWN = D // 4
DEPTH = 1024
SWAP = 1024
PART = COLS // 2
TILES = 2 * STEPS
UNITS = 4 * STEPS
PASS = 2
SHIP = UNITS - TILES + 5
AHEAD = 4

inner_rate = 2.0
outer_rate = 0.7
nesterov_coef = 0.9
epsilon = 1e-06
MESH = pl.DeviceIdType.MESH


def kernel(
    seg_ref, inp_ref, cot_ref, base_ref, mom_ref,
    nb_out, nm_out, w_out,
    xg, ysend, cot, base, mom, acc, keep, xs, xr, ps, rr, wt, segs, weight,
    load_sem, in_sem, seg_send, seg_recv,
    a1s, a1r, a2s, a2r, a3s, a3r, b1s, b1r, b2s, b2r, b3s, b3r, ys, yr, cots, cotr,
    xss, xsr, pss, psr, wcs, wcr, wls, wlr, wfs, wfr, out_sem,
):
    rep, f = lax.axis_index("replica"), lax.axis_index("fsdp")
    lo, core = rep // 2, rep % 2
    z, x, h = f // 8, (f // 2) % 4, f % 2

    def dev(x_=x, z_=z, h_=h, lo_=lo, core_=core):
        return (lo_ * 2 + core_, z_ * 8 + x_ * 2 + h_)

    def rot(v, d):
        return lax.rem(v + d, SIDE)

    other_core = dev(core_=1 - core)
    other_lo = dev(lo_=1 - lo)
    other_h = dev(h_=1 - h)
    along_x = [dev(x_=rot(x, d)) for d in (1, 2, 3)]
    along_z = [dev(z_=rot(z, d)) for d in (1, 2, 3)]

    def remote(src, dst, ss, rs, to):
        return pltpu.make_async_remote_copy(
            src_ref=src, dst_ref=dst, send_sem=ss, recv_sem=rs, device_id=to, device_id_type=MESH
        )

    def lanes(at, size=BLOCK):
        return pl.ds(pl.multiple_of(at, BLOCK), size)

    def load_rows(s, part, half):
        hh = h if half == 0 else 1 - h
        dst = xg.at[s, z, x, h] if half == 0 else ysend.at[s]
        return pltpu.make_async_copy(
            inp_ref.at[:, lanes(hh * HALF + part * OWN + s * BLOCK)],
            dst.at[:, part * BLOCK : (part + 1) * BLOCK],
            in_sem.at[s, part, half],
        )

    def load_all(s, carry):
        for part in (0, 1):
            for half in (0, 1):
                load_rows(s, part, half).start()
        return carry

    lax.fori_loop(0, STEPS, load_all, 0)
    def load_cot(u):
        return pltpu.make_async_copy(cot_ref.at[u * PART : (u + 1) * PART], cot.at[u], load_sem.at[2 + u])

    load_base = pltpu.make_async_copy(base_ref, base, load_sem.at[0])
    load_mom = pltpu.make_async_copy(mom_ref, mom, load_sem.at[1])
    segs[z, x, h] = jnp.broadcast_to(seg_ref[...], (8, TOK))

    barrier = pltpu.get_barrier_semaphore()
    partners = along_x + along_z + [other_core, other_lo, other_h, dev(h_=1 - h, lo_=1 - lo)]
    for to in partners:
        pl.semaphore_signal(barrier, inc=1, device_id=to, device_id_type=MESH)
    pl.semaphore_wait(barrier, len(partners))

    seg_h = remote(segs.at[z, x, h], segs.at[z, x, h], seg_send.at[2, 0], seg_recv.at[2, 0], other_h)

    def seg_x(d):
        return remote(segs.at[z, x], segs.at[z, x], seg_send.at[0, d], seg_recv.at[0, d], along_x[d])

    def seg_z(d):
        return remote(segs.at[z], segs.at[z], seg_send.at[1, d], seg_recv.at[1, d], along_z[d])

    def cross(s):
        return remote(ysend.at[s], xg.at[s, z, x, h], ys.at[s], yr.at[s], other_h)

    def a1(s, d):
        ref = xg.at[s, z, x, h]
        return remote(ref, ref, a1s.at[s, d], a1r.at[s, d], along_x[d])

    def a2(s, d):
        ref = xg.at[s, z, :, h]
        return remote(ref, ref, a2s.at[s, d], a2r.at[s, d], along_z[2 * d])

    def a3(s, d):
        ref = xg.at[s, rot(z, 3 - 2 * d), 2 * d : 2 * d + 2, h]
        return remote(ref, ref, a3s.at[s, d], a3r.at[s, d], along_z[2 * d])

    def b1(s, d):
        ref = xg.at[s, z, x, 1 - h]
        return remote(ref, ref, b1s.at[s, d], b1r.at[s, d], along_z[d])

    def b2(s, d):
        ref = xg.at[s, :, x, 1 - h]
        return remote(ref, ref, b2s.at[s, d], b2r.at[s, d], along_x[2 * d])

    def b3(s, d):
        ref = xg.at[s, 2 * d : 2 * d + 2, rot(x, 3 - 2 * d), 1 - h]
        return remote(ref, ref, b3s.at[s, d], b3r.at[s, d], along_x[2 * d])

    seg_h.start()

    def first(s, carry):
        for part in (0, 1):
            load_rows(s, part, 1).wait()
        cross(s).start()
        return carry

    def start_own(s):
        for part in (0, 1):
            load_rows(s, part, 0).wait()
        for d in range(3):
            a1(s, d).start()

    def tick(i):
        def at(s, body):
            @pl.when((s >= 0) & (s < STEPS))
            def _():
                body(s)

        def own2(s):
            for d in range(3):
                a1(s, d).wait_recv()
            for d in range(2):
                a2(s, d).start()

        def partner1(s):
            cross(s).wait_recv()
            for d in range(3):
                b1(s, d).start()

        def own3(s):
            for d in range(2):
                a2(s, d).wait_recv()
            for d in range(2):
                a3(s, d).start()

        def partner2(s):
            for d in range(3):
                b1(s, d).wait_recv()
            for d in range(2):
                b2(s, d).start()

        def partner3(s):
            for d in range(2):
                b2(s, d).wait_recv()
            for d in range(2):
                b3(s, d).start()

        at(i + 1, start_own)
        at(i - 1, own2)
        at(i - 1, partner1)
        at(i - 2, own3)
        at(i - 2, partner2)
        at(i - 3, partner3)

    start_own(0)
    lax.fori_loop(0, STEPS, first, 0)

    def send_cot(u):
        def go(i, carry):
            at = lanes(i * SWAP, SWAP)
            remote(cot_ref.at[u * PART : (u + 1) * PART, at], cot.at[2 + u, :, at], cots.at[u], cotr.at[u], other_h).start()
            return carry

        lax.fori_loop(0, TOK_G // SWAP, go, 0)

    send_cot(0)
    send_cot(1)
    seg_h.wait_recv()
    for d in range(3):
        seg_x(d).start()
    tick(0)
    load_cot(0).start()
    load_cot(1).start()
    load_base.start()
    load_mom.start()
    for d in range(3):
        seg_x(d).wait_recv()
    for d in range(3):
        seg_z(d).start()
    tick(1)
    tick(2)
    for d in range(3):
        seg_z(d).wait_recv()
    tick(3)

    ids = segs[...].reshape(TOK_G // TOK, 8, TOK)
    per_token = jnp.zeros((TOK_G // TOK, 8, TOK), jnp.float32)
    for doc in range(DOCS):
        mine = (ids == doc).astype(jnp.float32)
        count = jnp.sum(jnp.sum(mine, axis=0), axis=1, keepdims=True)
        per_token = per_token + mine * (1.0 / count)[None]
    weight[...] = per_token

    def scale_cot(g):
        def tile(i, carry):
            at = lanes(i * TOK)
            raw = cot[g, :, at].astype(jnp.float32).reshape(PART // 8, 8, TOK)
            cot[g, :, at] = (raw * weight[i][None]).reshape(PART, TOK).astype(jnp.bfloat16)
            return carry

        lax.fori_loop(0, TOK_G // TOK, tile, 0)

    for u in (0, 1):
        load_cot(u).wait()
        scale_cot(u)

    def swap(j):
        return remote(xs.at[j], xr.at[j], xss.at[j], xsr.at[j], other_core)

    def to_owner(j, g, s):
        c = jnp.where(g < 2, h, 1 - h)
        k = (g % 2) * STEPS + s
        return remote(ps.at[j], rr.at[k, lo], pss.at[j], psr.at[k, lo], dev(h_=c, lo_=h))

    def from_owner(k, src):
        return remote(ps.at[0], rr.at[k, src], pss.at[0], psr.at[k, src], other_lo)

    def place(k, ref, rp=None):
        u, s = k // STEPS, k % STEPS
        first = s * BLOCK if rp is None else rp * OWN + s * BLOCK
        return ref.at[pl.ds(pl.multiple_of(u * PART, 32), PART), lanes(first)]

    def w_core(k):
        return remote(wt.at[k], place(k, w_out, rep), wcs.at[k], wcr.at[k], other_core)

    def w_lo(k):
        return remote(wt.at[k], place(k, w_out, rep), wls.at[k], wlr.at[k], other_lo)

    def w_fwd(k):
        there = place(k, w_out, (1 - lo) * 2 + core)
        return remote(there, there, wfs.at[k], wfr.at[k], other_core)

    def w_own(k):
        return pltpu.make_async_copy(wt.at[k], place(k, w_out, rep), out_sem.at[0, k])

    def nm_own(k):
        return pltpu.make_async_copy(place(k, mom), place(k, nm_out), out_sem.at[1, k])

    def nb_own(k):
        return pltpu.make_async_copy(place(k, base), place(k, nb_out), out_sem.at[2, k])

    def quantized(at):
        blk = inner_rate * acc[:, lanes(at * BLOCK)]
        scale = (jnp.max(jnp.abs(blk), axis=1, keepdims=True) + epsilon).astype(jnp.bfloat16)
        scale = scale.astype(jnp.float32)
        coded = (blk * (1.0 / scale)).astype(jnp.bfloat16)
        return coded.astype(jnp.float32) * scale

    def unit(j):
        t = j - 15
        g = jnp.where(j < 10, j % 2, jnp.where(j < 15, 2, jnp.where(j < 24, t % 3, 3)))
        s = jnp.where(j < 10, j // 2, jnp.where(j < 15, j - 10, jnp.where(j < 24, 5 + t // 3, j - 24)))
        return g, s

    def step(j, carry):
        @pl.when(j < UNITS)
        def _():
            g, s = unit(j)

            @pl.when(g == 0)
            def _():
                tick(s + AHEAD)
                for d in range(2):
                    a3(s, d).wait_recv()
                    b3(s, d).wait_recv()

            for u, at in ((0, 10), (1, 24)):

                @pl.when(j == at)
                def _():
                    got = cot.at[2 + u]
                    pltpu.make_async_copy(got, got, cotr.at[u]).wait()
                    scale_cot(2 + u)

            def part(k, c):
                prod = jnp.dot(
                    cot[g, :, lanes(k * DEPTH, DEPTH)],
                    xg[s, k].reshape(DEPTH, 2 * BLOCK),
                    preferred_element_type=jnp.float32,
                )

                @pl.when(k == 0)
                def _():
                    acc[...] = prod

                @pl.when(k > 0)
                def _():
                    acc[...] += prod

                return c

            lax.fori_loop(0, TOK_G // DEPTH, part, 0)
            xs[j] = quantized(1 - core)
            swap(j).start()
            keep[j % 4] = quantized(core)

        @pl.when((j >= PASS) & (j < UNITS + PASS))
        def _():
            q = j - PASS
            g, s = unit(q)
            swap(q).wait_recv()
            ps[q] = (keep[q % 4] + xr[q]).astype(jnp.bfloat16)
            local = (g < 2) & (lo == h)

            @pl.when(local)
            def _():
                rr[g * STEPS + s, lo] = ps[q]

            @pl.when(jnp.logical_not(local))
            def _():
                to_owner(q, g, s).start()

        @pl.when(j == SHIP)
        def _():
            load_base.wait()
            load_mom.wait()

        @pl.when((j >= SHIP) & (j < SHIP + TILES))
        def _():
            k = j - SHIP
            from_owner(k, 1 - lo).wait_recv()

            @pl.when(lo != h)
            def _():
                from_owner(k, lo).wait_recv()

            average = (rr[k, 0].astype(jnp.float32) + rr[k, 1].astype(jnp.float32)) * 0.25
            u, s = k // STEPS, k % STEPS
            cols, at = pl.ds(pl.multiple_of(u * PART, 32), PART), lanes(s * BLOCK)
            nm = nesterov_coef * mom[cols, at] + average
            nb = base[cols, at] - outer_rate * (average + nesterov_coef * nm)
            wt[k] = nb.astype(jnp.bfloat16)
            w_lo(k).start()
            w_core(k).start()
            mom[cols, at] = nm
            base[cols, at] = nb
            w_own(k).start()
            nm_own(k).start()
            nb_own(k).start()

        @pl.when(j >= SHIP + 3)
        def _():
            k = j - (SHIP + 3)
            w_lo(k).wait_recv()
            w_fwd(k).start()

        return carry

    lax.fori_loop(0, SHIP + 3 + TILES, step, 0)

    for d in range(3):
        seg_x(d).wait_send()
        seg_z(d).wait_send()
    seg_h.wait_send()

    def finish(s, carry):
        for d in range(3):
            a1(s, d).wait_send()
            b1(s, d).wait_send()
        for d in range(2):
            a2(s, d).wait_send()
            b2(s, d).wait_send()
            a3(s, d).wait_send()
            b3(s, d).wait_send()
        cross(s).wait_send()
        return carry

    lax.fori_loop(0, STEPS, finish, 0)

    def finish_units(q, carry):
        g, s = unit(q)
        swap(q).wait_send()

        @pl.when(jnp.logical_not((g < 2) & (lo == h)))
        def _():
            to_owner(q, g, s).wait_send()

        return carry

    lax.fori_loop(0, UNITS, finish_units, 0)
    for u in (0, 1):
        pltpu.make_async_copy(cot.at[2 + u], cot.at[2 + u], cots.at[u]).wait()

    def finish_tiles(k, carry):
        w_core(k).wait_send()
        w_lo(k).wait_send()
        w_own(k).wait()
        nm_own(k).wait()
        nb_own(k).wait()
        w_core(k).wait_recv()
        w_fwd(k).wait_send()
        w_fwd(k).wait_recv()
        return carry

    lax.fori_loop(0, TILES, finish_tiles, 0)


def body(inputs, segments, cotangent, base, momentum):
    bf, f32, dma = jnp.bfloat16, jnp.float32, pltpu.SemaphoreType.DMA
    hbm = pl.BlockSpec(memory_space=pl.ANY)
    nb, nm, w = pl.pallas_call(
        kernel,
        out_shape=(
            jax.ShapeDtypeStruct((COLS, OWN), f32),
            jax.ShapeDtypeStruct((COLS, OWN), f32),
            jax.ShapeDtypeStruct((COLS, D), bf),
        ),
        in_specs=[pl.BlockSpec(memory_space=pltpu.VMEM), hbm, hbm, hbm, hbm],
        out_specs=(hbm, hbm, hbm),
        scratch_shapes=[
            pltpu.VMEM((STEPS, SIDE, SIDE, 2, TOK, 2 * BLOCK), bf),
            pltpu.VMEM((STEPS, TOK, 2 * BLOCK), bf),
            pltpu.VMEM((4, PART, TOK_G), bf),
            pltpu.VMEM((COLS, OWN), f32),
            pltpu.VMEM((COLS, OWN), f32),
            pltpu.VMEM((PART, 2 * BLOCK), f32),
            pltpu.VMEM((4, PART, BLOCK), f32),
            pltpu.VMEM((UNITS, PART, BLOCK), f32),
            pltpu.VMEM((UNITS, PART, BLOCK), f32),
            pltpu.VMEM((UNITS, PART, BLOCK), bf),
            pltpu.VMEM((TILES, 2, PART, BLOCK), bf),
            pltpu.VMEM((TILES, PART, BLOCK), bf),
            pltpu.VMEM((SIDE, SIDE, 2, 8, TOK), jnp.int32),
            pltpu.VMEM((TOK_G // TOK, 8, TOK), f32),
            dma((4,)), dma((STEPS, 2, 2)), dma((3, 3)), dma((3, 3)),
            dma((STEPS, 3)), dma((STEPS, 3)), dma((STEPS, 2)), dma((STEPS, 2)), dma((STEPS, 2)), dma((STEPS, 2)),
            dma((STEPS, 3)), dma((STEPS, 3)), dma((STEPS, 2)), dma((STEPS, 2)), dma((STEPS, 2)), dma((STEPS, 2)),
            dma((STEPS,)), dma((STEPS,)), dma((2,)), dma((2,)),
            dma((UNITS,)), dma((UNITS,)), dma((UNITS,)), dma((TILES, 2)),
            dma((TILES,)), dma((TILES,)), dma((TILES,)), dma((TILES,)),
            dma((TILES,)), dma((TILES,)), dma((3, TILES)),
        ],
        compiler_params=pltpu.CompilerParams(
            collective_id=0, has_side_effects=True, vmem_limit_bytes=60 * 2**20
        ),
        cost_estimate=pl.CostEstimate(flops=2 * D * D * COLS, bytes_accessed=2**24, transcendentals=0),
    )(segments, inputs[0], cotangent[0].T, base.T, momentum.T)
    return nb.T, nm.T, w.T


def solution(mesh):
    return jax.shard_map(
        body,
        mesh=mesh,
        in_specs=(
            P("replica", "fsdp", None),
            P("replica", "fsdp"),
            P("replica", None, "fsdp"),
            P("replica", "fsdp"),
            P("replica", "fsdp"),
        ),
        out_specs=(P("replica", "fsdp"), P("replica", "fsdp"), P(None, "fsdp")),
        check_vma=False,
    )
```

time: 620 us -> 171 us (0.28)
  waiting for transfers between devices: 451 us -> 0 us
  Pallas kernels: 0 us -> 163 us
  blocking collectives: 84.6 us -> 0 us
  other arithmetic: 31.7 us -> 0 us
  matrix products: 24.8 us -> 0 us
  between operations: 13.8 us -> 0.65 us
    all_gather x2 -> x0, waiting for transfers between devices: 310 us -> none  [the longest x1 267 us: body(): lax.all_gather(weighted, 'fsdp', axis=0, tiled=True)]
    pallas_call x0 -> x1, Pallas kernels: none -> 163 us  [body(): pl.pallas_call(kernel, out_shape=(jax.ShapeDtypeStruct((COLS, OWN), f32),...]
    psum x1 -> x0, waiting for transfers between devices: 141 us -> none  [body(): summed = lax.psum(decoded, 'replica')]
    psum x1 -> x0, blocking collectives: 84.6 us -> none  [body(): count = lax.psum(jnp.sum(onehot, axis=0), 'fsdp')]
    dot_general x2 -> x0, matrix products: 24.8 us -> none  [the longest x1 24.1 us: body(): lax.dot_general(lax.all_gather(weighted, 'fsdp', axis=0, tiled=True), loc...]
    mul x1 -> x0, other arithmetic: 13.5 us -> none  [body(): coded.astype(jnp.float32) * scale[:, None, :].astype(jnp.float32)]
    convert_element_type x3 -> x0, other arithmetic: 7.58 us -> none  [the longest x1 5.1 us: body(): new_base.astype(jnp.bfloat16)]
  transfers between devices with their start and end apart: 3 -> 0, of which waited for: 3 -> 0; matrix products, arithmetic and copies ran while one was open for 0% -> 0% of each run, Pallas kernels for 0% -> 0%
where the time goes in v2:
time: 171 us
  Pallas kernels  163 us (95%)
  local copies, waits for them, and re-layouts  7.61 us (4%)
    pallas_call x1, Pallas kernels, body(): pl.pallas_call(kernel, out_shape=(jax.ShapeDtypeStruct((COLS, OWN), f32),...  163 us
    unnamed x7, local copies, waits for them, and re-layouts  7.61 us

profile of v2, /device:TPU:1, one launch (start us, length us, event | category | flops | bytes accessed | tf_op | source)
XLA Modules:
  0.0 171.1 jit_solution(8233902903074401928)
XLA Ops:
  0.6 162.9 %shard_map.76 = (f32[448,1024]{1,0:T(8,128)}, f32[448,1024]{1,0:T(8,128)}, bf16[448,4096]{1,0:T(8,128)(2,1)}) custom-call(s32[1,128]{1,0:T(1,128)} %seg_ref.1, bf16[128,4096]{1,0:T(8,128)(2,1)} %bitcast.15, bf16[448,4096]{1,0:T(8,128)(2,1)} %bitcast.12, f32[448,1024]{1,0:T(8,128)} %bitcast.13, f32[448,1024]{1,0:T(8,128)} %bitcast.14), custom_call_target="tpu_custom_call" | custom-call | flops 15032385536 | bytes 16777216 | tf_op jit(solution)/shard_map/pallas_call | solution.py:432
  163.5 0.0 copy-start.1
  163.5 3.1 %copy.11 = f32[1024,448]{0,1:T(8,128)} copy(f32[1024,448]{0,1:T(8,128)} %bitcast.11) | data formatting | bytes 3670016
  166.6 0.0 copy-done.1
  166.6 0.0 copy-start
  166.6 1.2 copy.12
  167.8 1.5 copy-done
  169.3 1.8 %copy.13 = bf16[4096,448]{0,1:T(8,128)(2,1)} copy(bf16[4096,448]{0,1:T(8,128)(2,1)S(1)} %bitcast.9) | data formatting | bytes 7340032
Async XLA Ops:
  163.5 3.1 %copy-start.1 = (f32[448,1024]{1,0:T(8,128)S(1)}, f32[448,1024]{1,0:T(8,128)}, u32[]{:S(2)}) copy-start(f32[448,1024]{1,0:T(8,128)} %get-tuple-element.7) | copy-start | bytes 5505028
  166.6 2.7 %copy-start = (bf16[448,4096]{1,0:T(8,128)(2,1)S(1)}, bf16[448,4096]{1,0:T(8,128)(2,1)}, u32[]{:S(2)}) copy-start(bf16[448,4096]{1,0:T(8,128)(2,1)} %get-tuple-element.8) | copy-start | bytes 11010052

commit v3 on v2

v3 whole, which is shorter than its diff:
```python
import jax
import jax.numpy as jnp
from jax import lax
from jax.experimental import pallas as pl
from jax.experimental.pallas import tpu as pltpu
from jax.sharding import PartitionSpec as P

D = 4096
BLOCK = 128
DOCS = 16
STEPS = 8
SIDE = 4
TOK = 128
TOK_G = 4096
COLS = 448
HALF = D // 2
OWN = D // 4
DEPTH = 1024
SWAP = 1024
PART = COLS // 2
TILES = 2 * STEPS
UNITS = 4 * STEPS
PASS = 2
SHIP = UNITS - TILES + 5
AHEAD = 3

inner_rate = 2.0
outer_rate = 0.7
nesterov_coef = 0.9
epsilon = 1e-06
MESH = pl.DeviceIdType.MESH


def kernel(
    seg_ref, inp_ref, cot_ref, base_ref, mom_ref,
    nb_out, nm_out, w_out,
    xg, ysend, raw, cot, base, mom, acc, keep, xs, xr, ps, rr, wt, seg_own, segs, weight,
    load_sem, in_sem, seg_send, seg_recv,
    a1s, a1r, a2s, a2r, a3s, a3r, b1s, b1r, b2s, b2r, b3s, b3r, ys, yr, cots, cotr, rawr, fwds,
    xss, xsr, pss, psr, wcs, wcr, wls, wlr, wfs, wfr, out_sem,
):
    rep, f = lax.axis_index("replica"), lax.axis_index("fsdp")
    lo, core = rep // 2, rep % 2
    z, x, h = f // 8, (f // 2) % 4, f % 2

    def dev(x_=x, z_=z, h_=h, lo_=lo, core_=core):
        return (lo_ * 2 + core_, z_ * 8 + x_ * 2 + h_)

    def rot(v, d):
        return lax.rem(v + d, SIDE)

    other_core = dev(core_=1 - core)
    other_lo = dev(lo_=1 - lo)
    other_h = dev(h_=1 - h)
    across = dev(h_=1 - h, lo_=1 - lo)
    at_home = (h + core) % 2 == 0
    helper = dev(h_=jnp.where(at_home, 1 - h, h), lo_=1 - lo)
    along_x = [dev(x_=rot(x, d)) for d in (1, 2, 3)]
    along_z = [dev(z_=rot(z, d)) for d in (1, 2, 3)]

    def remote(src, dst, ss, rs, to):
        return pltpu.make_async_remote_copy(
            src_ref=src, dst_ref=dst, send_sem=ss, recv_sem=rs, device_id=to, device_id_type=MESH
        )

    def lanes(at, size=BLOCK):
        return pl.ds(pl.multiple_of(at, BLOCK), size)

    def load_rows(s, part, half, stay=False):
        hh = lo if half == 0 else 1 - lo
        dst = xg.at[s, z, x, h] if stay else ysend.at[half, s]
        return pltpu.make_async_copy(
            inp_ref.at[:, lanes(hh * HALF + part * OWN + s * BLOCK)],
            dst.at[:, part * BLOCK : (part + 1) * BLOCK],
            in_sem.at[s, part, half],
        )

    def load_all(s, carry):
        for part in (0, 1):
            load_rows(s, part, 0).start()

            @pl.when(at_home)
            def _():
                load_rows(s, part, 1, True).start()

            @pl.when(jnp.logical_not(at_home))
            def _():
                load_rows(s, part, 1).start()

        return carry

    lax.fori_loop(0, STEPS, load_all, 0)
    def load_cot(u):
        return pltpu.make_async_copy(cot_ref.at[u * PART : (u + 1) * PART], raw.at[u], load_sem.at[2 + u])

    load_base = pltpu.make_async_copy(base_ref, base, load_sem.at[0])
    load_mom = pltpu.make_async_copy(mom_ref, mom, load_sem.at[1])
    seg_own[...] = jnp.broadcast_to(seg_ref[...], (8, TOK))

    @pl.when(at_home)
    def _():
        segs[z, x, h] = jnp.broadcast_to(seg_ref[...], (8, TOK))

    barrier = pltpu.get_barrier_semaphore()
    partners = along_x + along_z + [other_core, other_lo, other_h, across]
    for to in partners:
        pl.semaphore_signal(barrier, inc=1, device_id=to, device_id_type=MESH)
    pl.semaphore_wait(barrier, len(partners))

    far = jnp.where(at_home, 0, 1)

    def seg_help(kind):
        return remote(seg_own, segs.at[z, x, h], seg_send.at[2, 0], seg_recv.at[2, kind], helper)

    seg_native = remote(seg_own, segs.at[z, x, h], seg_send.at[2, 1], seg_recv.at[2, 0], other_h)

    def seg_x(d):
        return remote(segs.at[z, x], segs.at[z, x], seg_send.at[0, d], seg_recv.at[0, d], along_x[d])

    def seg_z(d):
        return remote(segs.at[z], segs.at[z], seg_send.at[1, d], seg_recv.at[1, d], along_z[d])

    def cross_help(s, kind):
        return remote(ysend.at[0, s], xg.at[s, z, x, h], ys.at[0], yr.at[s, kind], helper)

    def cross_native(s):
        return remote(ysend.at[1, s], xg.at[s, z, x, h], ys.at[1], yr.at[s, 0], other_h)

    def a1(s, d):
        ref = xg.at[s, z, x, h]
        return remote(ref, ref, a1s, a1r.at[s, d], along_x[d])

    def a2(s, d):
        ref = xg.at[s, z, :, h]
        return remote(ref, ref, a2s, a2r.at[s, d], along_z[2 * d])

    def a3(s, d):
        ref = xg.at[s, rot(z, 3 - 2 * d), 2 * d : 2 * d + 2, h]
        return remote(ref, ref, a3s, a3r.at[s, d], along_z[2 * d])

    def b1(s, d):
        ref = xg.at[s, z, x, 1 - h]
        return remote(ref, ref, b1s, b1r.at[s, d], along_z[d])

    def b2(s, d):
        ref = xg.at[s, :, x, 1 - h]
        return remote(ref, ref, b2s, b2r.at[s, d], along_x[2 * d])

    def b3(s, d):
        ref = xg.at[s, 2 * d : 2 * d + 2, rot(x, 3 - 2 * d), 1 - h]
        return remote(ref, ref, b3s, b3r.at[s, d], along_x[2 * d])

    def away(body):
        pl.when(jnp.logical_not(at_home))(body)

    seg_help(far).start()
    away(lambda: seg_native.start())

    def first(s, carry):
        for part in (0, 1):
            load_rows(s, part, 0).wait()
        cross_help(s, far).start()

        @pl.when(jnp.logical_not(at_home))
        def _():
            for part in (0, 1):
                load_rows(s, part, 1).wait()
            cross_native(s).start()

        return carry

    def start_own(s):
        @pl.when(at_home)
        def _():
            for part in (0, 1):
                load_rows(s, part, 1, True).wait()

        @pl.when(jnp.logical_not(at_home))
        def _():
            cross_help(s, 1).wait_recv()

        for d in range(3):
            a1(s, d).start()

    def partner1(s):
        cross_help(s, 0).wait_recv()
        for d in range(3):
            b1(s, d).start()

    def tick(i):
        def at(s, body):
            @pl.when((s >= 0) & (s < STEPS))
            def _():
                body(s)

        def own2(s):
            for d in range(3):
                a1(s, d).wait_recv()
            for d in range(2):
                a2(s, d).start()

        def own3(s):
            for d in range(2):
                a2(s, d).wait_recv()
            for d in range(2):
                a3(s, d).start()

        def partner2(s):
            for d in range(3):
                b1(s, d).wait_recv()
            for d in range(2):
                b2(s, d).start()

        def partner3(s):
            for d in range(2):
                b2(s, d).wait_recv()
            for d in range(2):
                b3(s, d).start()

        at(i - 2, own3)
        at(i - 2, partner3)
        at(i - 1, own2)
        at(i - 1, partner2)
        at(i + 1, partner1)
        at(i + 3, start_own)

    def send_cot(u):
        @pl.when(at_home)
        def _():
            def go(i, carry):
                at = lanes(i * SWAP, SWAP)
                remote(cot_ref.at[u * PART : (u + 1) * PART, at], cot.at[2 + u, :, at], cots.at[u], cotr.at[u], across).start()
                return carry

            lax.fori_loop(0, TOK_G // SWAP, go, 0)

        @pl.when(jnp.logical_not(at_home))
        def _():
            def go(i, carry):
                at = lanes(i * SWAP, SWAP)
                remote(cot_ref.at[u * PART : (u + 1) * PART, at], raw.at[u, :, at], cots.at[u], rawr.at[u, i], other_lo).start()
                return carry

            lax.fori_loop(0, TOK_G // SWAP, go, 0)

    def pass_cot(u, first, last):
        @pl.when(jnp.logical_not(at_home))
        def _():
            def go(i, carry):
                at = lanes(i * SWAP, SWAP)
                remote(raw.at[u, :, at], raw.at[u, :, at], cots.at[u], rawr.at[u, i], other_lo).wait_recv()
                remote(raw.at[u, :, at], cot.at[2 + u, :, at], fwds.at[u], cotr.at[u], across).start()
                return carry

            lax.fori_loop(first, last, go, 0)

    lax.fori_loop(0, STEPS, first, 0)
    send_cot(0)
    send_cot(1)
    start_own(0)
    partner1(0)
    start_own(1)
    start_own(2)
    seg_help(0).wait_recv()
    away(lambda: seg_help(1).wait_recv())
    for d in range(3):
        seg_x(d).start()
    tick(0)

    @pl.when(at_home)
    def _():
        load_cot(0).start()
        load_cot(1).start()

    load_base.start()
    load_mom.start()
    for d in range(3):
        seg_x(d).wait_recv()
    for d in range(3):
        seg_z(d).start()
    tick(1)
    tick(2)
    for d in range(3):
        seg_z(d).wait_recv()
    pass_cot(0, 0, 2)
    tick(3)
    pass_cot(0, 2, TOK_G // SWAP)

    ids = segs[...].reshape(TOK_G // TOK, 8, TOK)
    per_token = jnp.zeros((TOK_G // TOK, 8, TOK), jnp.float32)
    for doc in range(DOCS):
        mine = (ids == doc).astype(jnp.float32)
        count = jnp.sum(jnp.sum(mine, axis=0), axis=1, keepdims=True)
        per_token = per_token + mine * (1.0 / count)[None]
    weight[...] = per_token

    def scale_cot(src, g):
        def tile(i, carry):
            at = lanes(i * TOK)
            block = src[:, at].astype(jnp.float32).reshape(PART // 8, 8, TOK)
            cot[g, :, at] = (block * weight[i][None]).reshape(PART, TOK).astype(jnp.bfloat16)
            return carry

        lax.fori_loop(0, TOK_G // TOK, tile, 0)

    def scale_own(u):
        @pl.when(at_home)
        def _():
            load_cot(u).wait()

        scale_cot(raw.at[u], u)

    scale_own(0)

    def swap(j):
        return remote(xs.at[j], xr.at[j], xss, xsr.at[j], other_core)

    def to_owner(j, g, s):
        k, side = (g % 2) * STEPS + s, g // 2
        return remote(ps.at[j], rr.at[k, side], pss, psr.at[k, side], dev(h_=jnp.where(g < 2, h, 1 - h), lo_=1 - lo))

    def from_owner(k, side):
        return remote(ps.at[0], rr.at[k, side], pss, psr.at[k, side], other_lo)

    def place(k, ref, rp=None):
        u, s = k // STEPS, k % STEPS
        first = s * BLOCK if rp is None else rp * OWN + s * BLOCK
        return ref.at[pl.ds(pl.multiple_of(u * PART, 32), PART), lanes(first)]

    def w_core(k):
        return remote(wt.at[k], place(k, w_out, rep), wcs, wcr, other_core)

    def w_lo(k):
        return remote(wt.at[k], place(k, w_out, rep), wls, wlr.at[k], other_lo)

    def w_fwd(k):
        there = place(k, w_out, (1 - lo) * 2 + core)
        return remote(there, there, wfs, wfr, other_core)

    def w_own(k):
        return pltpu.make_async_copy(wt.at[k], place(k, w_out, rep), out_sem.at[0])

    def nm_own(k):
        return pltpu.make_async_copy(place(k, mom), place(k, nm_out), out_sem.at[1])

    def nb_own(k):
        return pltpu.make_async_copy(place(k, base), place(k, nb_out), out_sem.at[2])

    def quantized(at):
        blk = inner_rate * acc[:, lanes(at * BLOCK)]
        scale = (jnp.max(jnp.abs(blk), axis=1, keepdims=True) + epsilon).astype(jnp.bfloat16)
        scale = scale.astype(jnp.float32)
        coded = (blk * (1.0 / scale)).astype(jnp.bfloat16)
        return coded.astype(jnp.float32) * scale

    def pick(j, *cases):
        value = cases[-1]
        for bound, case in reversed(cases[:-1]):
            value = jnp.where(j < bound, case, value)
        return value

    def unit(j):
        g = pick(j, (6, j // 3), (10, j % 2), (15, 2), (21, j % 3), (27, 3), (30, j - 27), 3)
        s = pick(j, (6, j % 3), (10, j // 2), (15, j - 10), (21, j // 3), (27, j - 21), (30, STEPS - 1), j - 24)
        return g, s

    def tile_of(m):
        return pick(m, (7, m), (13, m + 1), (14, 7), m)

    def step(j, carry):
        @pl.when(j < UNITS)
        def _():
            g, s = unit(j)

            @pl.when(g == 0)
            def _():
                for d in range(2):
                    a3(s, d).wait_recv()
                    b3(s, d).wait_recv()

            @pl.when(j == 3)
            def _():
                pass_cot(1, 0, TOK_G // SWAP)
                scale_own(1)

            for u, at in ((0, 10), (1, 21)):

                @pl.when(j == at)
                def _():
                    got = cot.at[2 + u]
                    pltpu.make_async_copy(got, got, cotr.at[u]).wait()
                    scale_cot(got, 2 + u)

            def part(k, c):
                prod = jnp.dot(
                    cot[g, :, lanes(k * DEPTH, DEPTH)],
                    xg[s, k].reshape(DEPTH, 2 * BLOCK),
                    preferred_element_type=jnp.float32,
                )

                @pl.when(k == 0)
                def _():
                    acc[...] = prod

                @pl.when(k > 0)
                def _():
                    acc[...] += prod

                return c

            lax.fori_loop(0, TOK_G // DEPTH, part, 0)
            xs[j] = quantized(1 - core)
            swap(j).start()
            keep[j % 4] = quantized(core)

            @pl.when(((g == 0) & (s > 0) & (s < 3)) | ((g == 1) & (s >= 3)))
            def _():
                tick(s + AHEAD)

        @pl.when((j >= PASS) & (j < UNITS + PASS))
        def _():
            q = j - PASS
            g, s = unit(q)
            swap(q).wait_recv()
            ps[q] = (keep[q % 4] + xr[q]).astype(jnp.bfloat16)
            to_owner(q, g, s).start()

        @pl.when(j == SHIP)
        def _():
            load_base.wait()
            load_mom.wait()

        @pl.when((j >= SHIP) & (j < SHIP + TILES))
        def _():
            k = tile_of(j - SHIP)
            from_owner(k, 0).wait_recv()
            from_owner(k, 1).wait_recv()
            average = (rr[k, 0].astype(jnp.float32) + rr[k, 1].astype(jnp.float32)) * 0.25
            u, s = k // STEPS, k % STEPS
            cols, at = pl.ds(pl.multiple_of(u * PART, 32), PART), lanes(s * BLOCK)
            nm = nesterov_coef * mom[cols, at] + average
            nb = base[cols, at] - outer_rate * (average + nesterov_coef * nm)
            wt[k] = nb.astype(jnp.bfloat16)
            w_lo(k).start()
            w_core(k).start()
            mom[cols, at] = nm
            base[cols, at] = nb
            w_own(k).start()
            nm_own(k).start()
            nb_own(k).start()

        @pl.when(j >= SHIP + 3)
        def _():
            k = tile_of(j - (SHIP + 3))
            w_lo(k).wait_recv()
            w_fwd(k).start()

        return carry

    lax.fori_loop(0, SHIP + 3 + TILES, step, 0)

    for d in range(3):
        seg_x(d).wait_send()
        seg_z(d).wait_send()
    seg_help(far).wait_send()
    away(lambda: seg_native.wait_send())

    def drain(ref, sem):
        pltpu.make_async_copy(ref, ref, sem).wait()

    for sem in (a1s, b1s):
        drain(xg.at[0, :3], sem)
    for sem in (a2s, b2s):
        drain(xg.at[:2], sem)
    for sem in (a3s, b3s):
        drain(xg.at[:1], sem)
    drain(ysend.at[0], ys.at[0])
    away(lambda: drain(ysend.at[1], ys.at[1]))
    drain(xs, xss)
    drain(ps, pss)
    for u in (0, 1):
        pltpu.make_async_copy(cot.at[2 + u], cot.at[2 + u], cots.at[u]).wait()

        @pl.when(jnp.logical_not(at_home))
        def _():
            pltpu.make_async_copy(cot.at[2 + u], cot.at[2 + u], fwds.at[u]).wait()

    for sem in (wcs, wls, wfs, wcr, wfr, out_sem.at[0]):
        drain(wt, sem)
    drain(mom, out_sem.at[1])
    drain(base, out_sem.at[2])


def body(inputs, segments, cotangent, base, momentum):
    bf, f32, dma = jnp.bfloat16, jnp.float32, pltpu.SemaphoreType.DMA
    hbm = pl.BlockSpec(memory_space=pl.ANY)
    nb, nm, w = pl.pallas_call(
        kernel,
        out_shape=(
            jax.ShapeDtypeStruct((COLS, OWN), f32),
            jax.ShapeDtypeStruct((COLS, OWN), f32),
            jax.ShapeDtypeStruct((COLS, D), bf),
        ),
        in_specs=[pl.BlockSpec(memory_space=pltpu.VMEM), hbm, hbm, hbm, hbm],
        out_specs=(hbm, hbm, hbm),
        scratch_shapes=[
            pltpu.VMEM((STEPS, SIDE, SIDE, 2, TOK, 2 * BLOCK), bf),
            pltpu.VMEM((2, STEPS, TOK, 2 * BLOCK), bf),
            pltpu.VMEM((2, PART, TOK_G), bf),
            pltpu.VMEM((4, PART, TOK_G), bf),
            pltpu.VMEM((COLS, OWN), f32),
            pltpu.VMEM((COLS, OWN), f32),
            pltpu.VMEM((PART, 2 * BLOCK), f32),
            pltpu.VMEM((4, PART, BLOCK), f32),
            pltpu.VMEM((UNITS, PART, BLOCK), f32),
            pltpu.VMEM((UNITS, PART, BLOCK), f32),
            pltpu.VMEM((UNITS, PART, BLOCK), bf),
            pltpu.VMEM((TILES, 2, PART, BLOCK), bf),
            pltpu.VMEM((TILES, PART, BLOCK), bf),
            pltpu.VMEM((8, TOK), jnp.int32),
            pltpu.VMEM((SIDE, SIDE, 2, 8, TOK), jnp.int32),
            pltpu.VMEM((TOK_G // TOK, 8, TOK), f32),
            dma((4,)), dma((STEPS, 2, 2)), dma((3, 3)), dma((3, 3)),
            dma, dma((STEPS, 3)), dma, dma((STEPS, 2)), dma, dma((STEPS, 2)),
            dma, dma((STEPS, 3)), dma, dma((STEPS, 2)), dma, dma((STEPS, 2)),
            dma((2,)), dma((STEPS, 2)), dma((2,)), dma((2,)), dma((2, TOK_G // SWAP)), dma((2,)),
            dma, dma((UNITS,)), dma, dma((TILES, 2)),
            dma, dma, dma, dma((TILES,)), dma, dma, dma((3,)),
        ],
        compiler_params=pltpu.CompilerParams(
            collective_id=0, has_side_effects=True, vmem_limit_bytes=60 * 2**20
        ),
        cost_estimate=pl.CostEstimate(flops=2 * D * D * COLS, bytes_accessed=2**24, transcendentals=0),
    )(segments, inputs[0], cotangent[0].T, base.T, momentum.T)
    return nb.T, nm.T, w.T


def solution(mesh):
    return jax.shard_map(
        body,
        mesh=mesh,
        in_specs=(
            P("replica", "fsdp", None),
            P("replica", "fsdp"),
            P("replica", None, "fsdp"),
            P("replica", "fsdp"),
            P("replica", "fsdp"),
        ),
        out_specs=(P("replica", "fsdp"), P("replica", "fsdp"), P(None, "fsdp")),
        check_vma=False,
    )
```

time: 171 us -> 152 us (0.89)
  Pallas kernels: 163 us -> 144 us
    pallas_call x1, Pallas kernels: 163 us -> 144 us  [body(): pl.pallas_call(kernel, out_shape=(jax.ShapeDtypeStruct((COLS, OWN), f32),...]
where the time goes in v3:
time: 152 us
  Pallas kernels  144 us (95%)
  local copies, waits for them, and re-layouts  7.61 us (5%)
    pallas_call x1, Pallas kernels, body(): pl.pallas_call(kernel, out_shape=(jax.ShapeDtypeStruct((COLS, OWN), f32),...  144 us
    unnamed x7, local copies, waits for them, and re-layouts  7.61 us

profile of v3, /device:TPU:1, one launch (start us, length us, event | category | flops | bytes accessed | tf_op | source)
XLA Modules:
  0.0 152.0 jit_solution(10399579861517880068)
XLA Ops:
  0.6 143.8 %shard_map.76 = (f32[448,1024]{1,0:T(8,128)}, f32[448,1024]{1,0:T(8,128)}, bf16[448,4096]{1,0:T(8,128)(2,1)}) custom-call(s32[1,128]{1,0:T(1,128)} %seg_ref.1, bf16[128,4096]{1,0:T(8,128)(2,1)} %bitcast.15, bf16[448,4096]{1,0:T(8,128)(2,1)} %bitcast.12, f32[448,1024]{1,0:T(8,128)} %bitcast.13, f32[448,1024]{1,0:T(8,128)} %bitcast.14), custom_call_target="tpu_custom_call" | custom-call | flops 15032385536 | bytes 16777216 | tf_op jit(solution)/shard_map/pallas_call | solution.py:497
  144.4 0.0 copy-start.1
  144.4 3.1 %copy.11 = f32[1024,448]{0,1:T(8,128)} copy(f32[1024,448]{0,1:T(8,128)} %bitcast.11) | data formatting | bytes 3670016
  147.5 0.0 copy-done.1
  147.5 0.0 copy-start
  147.5 1.2 copy.12
  148.7 1.5 copy-done
  150.2 1.8 %copy.13 = bf16[4096,448]{0,1:T(8,128)(2,1)} copy(bf16[4096,448]{0,1:T(8,128)(2,1)S(1)} %bitcast.9) | data formatting | bytes 7340032
Async XLA Ops:
  144.4 3.1 %copy-start.1 = (f32[448,1024]{1,0:T(8,128)S(1)}, f32[448,1024]{1,0:T(8,128)}, u32[]{:S(2)}) copy-start(f32[448,1024]{1,0:T(8,128)} %get-tuple-element.7) | copy-start | bytes 5505028
  147.5 2.7 %copy-start = (bf16[448,4096]{1,0:T(8,128)(2,1)S(1)}, bf16[448,4096]{1,0:T(8,128)(2,1)}, u32[]{:S(2)}) copy-start(bf16[448,4096]{1,0:T(8,128)(2,1)} %get-tuple-element.8) | copy-start | bytes 11010052

commit v4 on v3

--- a/solution.py
+++ b/solution.py
@@ -15,13 +15,14 @@
 COLS = 448
 HALF = D // 2
 OWN = D // 4
-DEPTH = 1024
 SWAP = 1024
 PART = COLS // 2
 TILES = 2 * STEPS
 UNITS = 4 * STEPS
-PASS = 2
-SHIP = UNITS - TILES + 5
+PASS = 3
+DIRECT = 3
+STORES = 4
+SHIP = UNITS - TILES + 6
 AHEAD = 3
 
 inner_rate = 2.0
@@ -34,7 +35,7 @@
 def kernel(
     seg_ref, inp_ref, cot_ref, base_ref, mom_ref,
     nb_out, nm_out, w_out,
-    xg, ysend, raw, cot, base, mom, acc, keep, xs, xr, ps, rr, wt, seg_own, segs, weight,
+    xg, ysend, raw, cot, base, mom, acc, keep, xs, xr, ps, rr, wt, seg_row, seg_own, segs, weight,
     load_sem, in_sem, seg_send, seg_recv,
     a1s, a1r, a2s, a2r, a3s, a3r, b1s, b1r, b2s, b2r, b3s, b3r, ys, yr, cots, cotr, rawr, fwds,
     xss, xsr, pss, psr, wcs, wcr, wls, wlr, wfs, wfr, out_sem,
@@ -55,6 +56,7 @@
     across = dev(h_=1 - h, lo_=1 - lo)
     at_home = (h + core) % 2 == 0
     helper = dev(h_=jnp.where(at_home, 1 - h, h), lo_=1 - lo)
+    other_both = dev(lo_=1 - lo, core_=1 - core)
     along_x = [dev(x_=rot(x, d)) for d in (1, 2, 3)]
     along_z = [dev(z_=rot(z, d)) for d in (1, 2, 3)]
 
@@ -65,6 +67,14 @@
 
     def lanes(at, size=BLOCK):
         return pl.ds(pl.multiple_of(at, BLOCK), size)
+
+    barrier = pltpu.get_barrier_semaphore()
+    partners = along_x + along_z + [other_core, other_lo, other_h, across, other_both]
+    for to in partners:
+        pl.semaphore_signal(barrier, inc=1, device_id=to, device_id_type=MESH)
+
+    load_seg = pltpu.make_async_copy(seg_ref, seg_row, load_sem.at[4])
+    load_seg.start()
 
     def load_rows(s, part, half, stay=False):
         hh = lo if half == 0 else 1 - lo
@@ -95,16 +105,13 @@
 
     load_base = pltpu.make_async_copy(base_ref, base, load_sem.at[0])
     load_mom = pltpu.make_async_copy(mom_ref, mom, load_sem.at[1])
-    seg_own[...] = jnp.broadcast_to(seg_ref[...], (8, TOK))
+    load_seg.wait()
+    seg_own[...] = jnp.broadcast_to(seg_row[...], (8, TOK))
 
     @pl.when(at_home)
     def _():
-        segs[z, x, h] = jnp.broadcast_to(seg_ref[...], (8, TOK))
-
-    barrier = pltpu.get_barrier_semaphore()
-    partners = along_x + along_z + [other_core, other_lo, other_h, across]
-    for to in partners:
-        pl.semaphore_signal(barrier, inc=1, device_id=to, device_id_type=MESH)
+        segs[z, x, h] = jnp.broadcast_to(seg_row[...], (8, TOK))
+
     pl.semaphore_wait(barrier, len(partners))
 
     far = jnp.where(at_home, 0, 1)
@@ -337,6 +344,9 @@
         there = place(k, w_out, (1 - lo) * 2 + core)
         return remote(there, there, wfs, wfr, other_core)
 
+    def w_diag(k):
+        return remote(wt.at[k], place(k, w_out, rep), wfs, wfr, other_both)
+
     def w_own(k):
         return pltpu.make_async_copy(wt.at[k], place(k, w_out, rep), out_sem.at[0])
 
@@ -360,12 +370,12 @@
         return value
 
     def unit(j):
-        g = pick(j, (6, j // 3), (10, j % 2), (15, 2), (21, j % 3), (27, 3), (30, j - 27), 3)
-        s = pick(j, (6, j % 3), (10, j // 2), (15, j - 10), (21, j // 3), (27, j - 21), (30, STEPS - 1), j - 24)
+        g = pick(j, (6, j // 3), (10, j % 2), (15, 2), (21, j % 3), (28, 3), (31, j - 28), 3)
+        s = pick(j, (6, j % 3), (10, j // 2), (15, j - 10), (21, j // 3), (28, j - 21), STEPS - 1)
         return g, s
 
     def tile_of(m):
-        return pick(m, (7, m), (13, m + 1), (14, 7), m)
+        return pick(m, (7, m), (14, m + 1), (15, 7), m)
 
     def step(j, carry):
         @pl.when(j < UNITS)
@@ -391,24 +401,7 @@
                     pltpu.make_async_copy(got, got, cotr.at[u]).wait()
                     scale_cot(got, 2 + u)
 
-            def part(k, c):
-                prod = jnp.dot(
-                    cot[g, :, lanes(k * DEPTH, DEPTH)],
-                    xg[s, k].reshape(DEPTH, 2 * BLOCK),
-                    preferred_element_type=jnp.float32,
-                )
-
-                @pl.when(k == 0)
-                def _():
-                    acc[...] = prod
-
-                @pl.when(k > 0)
-                def _():
-                    acc[...] += prod
-
-                return c
-
-            lax.fori_loop(0, TOK_G // DEPTH, part, 0)
+            acc[...] = jnp.dot(cot[g], xg[s].reshape(TOK_G, 2 * BLOCK), preferred_element_type=jnp.float32)
             xs[j] = quantized(1 - core)
             swap(j).start()
             keep[j % 4] = quantized(core)
@@ -442,6 +435,11 @@
             nb = base[cols, at] - outer_rate * (average + nesterov_coef * nm)
             wt[k] = nb.astype(jnp.bfloat16)
             w_lo(k).start()
+
+            @pl.when(j >= SHIP + TILES - DIRECT)
+            def _():
+                w_diag(k).start()
+
             w_core(k).start()
             mom[cols, at] = nm
             base[cols, at] = nb
@@ -449,7 +447,7 @@
             nm_own(k).start()
             nb_own(k).start()
 
-        @pl.when(j >= SHIP + 3)
+        @pl.when((j >= SHIP + 3) & (j < SHIP + 3 + TILES - DIRECT))
         def _():
             k = tile_of(j - (SHIP + 3))
             w_lo(k).wait_recv()
@@ -457,7 +455,7 @@
 
         return carry
 
-    lax.fori_loop(0, SHIP + 3 + TILES, step, 0)
+    lax.fori_loop(0, SHIP + TILES, step, 0)
 
     for d in range(3):
         seg_x(d).wait_send()
@@ -487,8 +485,16 @@
 
     for sem in (wcs, wls, wfs, wcr, wfr, out_sem.at[0]):
         drain(wt, sem)
+    for m in range(TILES - DIRECT, TILES):
+        w_lo(tile_of(m)).wait_recv()
     drain(mom, out_sem.at[1])
     drain(base, out_sem.at[2])
+
+
+def store(nb, nm, w, nb_out, nm_out, w_out):
+    nb_out[...] = nb[...]
+    nm_out[...] = nm[...]
+    w_out[...] = w[...]
 
 
 def body(inputs, segments, cotangent, base, momentum):
@@ -501,7 +507,7 @@
             jax.ShapeDtypeStruct((COLS, OWN), f32),
             jax.ShapeDtypeStruct((COLS, D), bf),
         ),
-        in_specs=[pl.BlockSpec(memory_space=pltpu.VMEM), hbm, hbm, hbm, hbm],
+        in_specs=[hbm] * 5,
         out_specs=(hbm, hbm, hbm),
         scratch_shapes=[
             pltpu.VMEM((STEPS, SIDE, SIDE, 2, TOK, 2 * BLOCK), bf),
@@ -517,10 +523,11 @@
             pltpu.VMEM((UNITS, PART, BLOCK), bf),
             pltpu.VMEM((TILES, 2, PART, BLOCK), bf),
             pltpu.VMEM((TILES, PART, BLOCK), bf),
+            pltpu.VMEM((1, TOK), jnp.int32),
             pltpu.VMEM((8, TOK), jnp.int32),
             pltpu.VMEM((SIDE, SIDE, 2, 8, TOK), jnp.int32),
             pltpu.VMEM((TOK_G // TOK, 8, TOK), f32),
-            dma((4,)), dma((STEPS, 2, 2)), dma((3, 3)), dma((3, 3)),
+            dma((5,)), dma((STEPS, 2, 2)), dma((3, 3)), dma((3, 3)),
             dma, dma((STEPS, 3)), dma, dma((STEPS, 2)), dma, dma((STEPS, 2)),
             dma, dma((STEPS, 3)), dma, dma((STEPS, 2)), dma, dma((STEPS, 2)),
             dma((2,)), dma((STEPS, 2)), dma((2,)), dma((2,)), dma((2, TOK_G // SWAP)), dma((2,)),
@@ -532,6 +539,17 @@
         ),
         cost_estimate=pl.CostEstimate(flops=2 * D * D * COLS, bytes_accessed=2**24, transcendentals=0),
     )(segments, inputs[0], cotangent[0].T, base.T, momentum.T)
+    nb, nm, w = pl.pallas_call(
+        store,
+        out_shape=(
+            jax.ShapeDtypeStruct((COLS, OWN), f32),
+            jax.ShapeDtypeStruct((COLS, OWN), f32),
+            jax.ShapeDtypeStruct((COLS, D), bf),
+        ),
+        grid=(STORES,),
+        in_specs=[pl.BlockSpec((COLS // STORES, width), lambda i: (i, 0)) for width in (OWN, OWN, D)],
+        out_specs=tuple(pl.BlockSpec((COLS // STORES, width), lambda i: (i, 0)) for width in (OWN, OWN, D)),
+    )(nb, nm, w)
     return nb.T, nm.T, w.T
 
 

time: 152 us -> 147 us (0.967)
  local copies, waits for them, and re-layouts: 7.61 us -> 0 us
    unnamed x7 -> x0, local copies, waits for them, and re-layouts: 7.61 us -> none
    pallas_call x0 -> x1, Pallas kernels: none -> 6.44 us  [body(): pl.pallas_call(store, out_shape=(jax.ShapeDtypeStruct((COLS, OWN), f32),...]
    pallas_call x1, Pallas kernels: 144 us -> 139 us  [body(): pl.pallas_call(kernel, out_shape=(jax.ShapeDtypeStruct((COLS, OWN), f32),...]
where the time goes in v4:
time: 147 us; the launch traced here: 146 us
  Pallas kernels  145 us (99%)
    pallas_call x1, Pallas kernels, body(): pl.pallas_call(kernel, out_shape=(jax.ShapeDtypeStruct((COLS, OWN), f32),...  139 us
    pallas_call x1, Pallas kernels, body(): pl.pallas_call(store, out_shape=(jax.ShapeDtypeStruct((COLS, OWN), f32),...  6.44 us

profile of v4, /device:TPU:1, one launch (start us, length us, event | category | flops | bytes accessed | tf_op | source)
XLA Modules:
  0.0 145.9 jit_solution(17989537218709610327)
XLA Ops:
  0.6 138.8 %shard_map.76 = (f32[448,1024]{1,0:T(8,128)}, f32[448,1024]{1,0:T(8,128)}, bf16[448,4096]{1,0:T(8,128)(2,1)}) custom-call(s32[1,128]{1,0:T(1,128)} %seg_ref.1, bf16[128,4096]{1,0:T(8,128)(2,1)} %bitcast.15, bf16[448,4096]{1,0:T(8,128)(2,1)} %bitcast.9, f32[448,1024]{1,0:T(8,128)} %bitcast.11, f32[448,1024]{1,0:T(8,128)} %bitcast.12), custom_call_target="tpu_custom_call" | custom-call | flops 15032385536 | bytes 16777216 | tf_op jit(solution)/shard_map/pallas_call | solution.py:503
  139.5 6.4 %shard_map.77 = (f32[448,1024]{1,0:T(8,128)}, f32[448,1024]{1,0:T(8,128)}, bf16[448,4096]{1,0:T(8,128)(2,1)}) custom-call(f32[448,1024]{1,0:T(8,128)} %get-tuple-element.9.nb, f32[448,1024]{1,0:T(8,128)} %get-tuple-element.10.nm, bf16[448,4096]{1,0:T(8,128)(2,1)} %get-tuple-element.11.w), custom_call_target="tpu_custom_call" | custom-call | tf_op jit(solution)/shard_map/pallas_call | solution.py:542

commit v5 on v4

--- a/solution.py
+++ b/solution.py
@@ -19,11 +19,13 @@
 PART = COLS // 2
 TILES = 2 * STEPS
 UNITS = 4 * STEPS
-PASS = 3
-DIRECT = 3
+PASS = 1
+FWD = 3
+DIRECT = 1
 STORES = 4
-SHIP = UNITS - TILES + 6
+SHIP = UNITS - TILES + 2
 AHEAD = 3
+RELAYED = STEPS - 1
 
 inner_rate = 2.0
 outer_rate = 0.7
@@ -145,6 +147,14 @@
         ref = xg.at[s, rot(z, 3 - 2 * d), 2 * d : 2 * d + 2, h]
         return remote(ref, ref, a3s, a3r.at[s, d], along_z[2 * d])
 
+    def a_far(s):
+        ref = xg.at[s, z, :, h]
+        return remote(ref, ref, a3s, a3r.at[s, 0], along_z[1])
+
+    def b_far(s):
+        ref = xg.at[s, :, x, 1 - h]
+        return remote(ref, ref, b3s, b3r.at[s, 0], along_x[1])
+
     def b1(s, d):
         ref = xg.at[s, z, x, 1 - h]
         return remote(ref, ref, b1s, b1r.at[s, d], along_z[d])
@@ -195,8 +205,8 @@
             b1(s, d).start()
 
     def tick(i):
-        def at(s, body):
-            @pl.when((s >= 0) & (s < STEPS))
+        def at(s, body, end=STEPS):
+            @pl.when((s >= 0) & (s < end))
             def _():
                 body(s)
 
@@ -206,6 +216,10 @@
             for d in range(2):
                 a2(s, d).start()
 
+            @pl.when(s >= RELAYED)
+            def _():
+                a_far(s).start()
+
         def own3(s):
             for d in range(2):
                 a2(s, d).wait_recv()
@@ -218,14 +232,18 @@
             for d in range(2):
                 b2(s, d).start()
 
+            @pl.when(s >= RELAYED)
+            def _():
+                b_far(s).start()
+
         def partner3(s):
             for d in range(2):
                 b2(s, d).wait_recv()
             for d in range(2):
                 b3(s, d).start()
 
-        at(i - 2, own3)
-        at(i - 2, partner3)
+        at(i - 2, own3, RELAYED)
+        at(i - 2, partner3, RELAYED)
         at(i - 1, own2)
         at(i - 1, partner2)
         at(i + 1, partner1)
@@ -384,9 +402,19 @@
 
             @pl.when(g == 0)
             def _():
-                for d in range(2):
-                    a3(s, d).wait_recv()
-                    b3(s, d).wait_recv()
+                @pl.when(s < RELAYED)
+                def _():
+                    for d in range(2):
+                        a3(s, d).wait_recv()
+                        b3(s, d).wait_recv()
+
+                @pl.when(s >= RELAYED)
+                def _():
+                    for d in range(2):
+                        a2(s, d).wait_recv()
+                        b2(s, d).wait_recv()
+                    a_far(s).wait_recv()
+                    b_far(s).wait_recv()
 
             @pl.when(j == 3)
             def _():
@@ -447,15 +475,15 @@
             nm_own(k).start()
             nb_own(k).start()
 
-        @pl.when((j >= SHIP + 3) & (j < SHIP + 3 + TILES - DIRECT))
-        def _():
-            k = tile_of(j - (SHIP + 3))
+        @pl.when((j >= SHIP + FWD) & (j < SHIP + FWD + TILES - DIRECT))
+        def _():
+            k = tile_of(j - (SHIP + FWD))
             w_lo(k).wait_recv()
             w_fwd(k).start()
 
         return carry
 
-    lax.fori_loop(0, SHIP + TILES, step, 0)
+    lax.fori_loop(0, SHIP + TILES + max(0, FWD - DIRECT), step, 0)
 
     for d in range(3):
         seg_x(d).wait_send()

time: 147 us -> 140 us (0.952)
  Pallas kernels: 145 us -> 139 us
    pallas_call x1, Pallas kernels: 139 us -> 133 us  [body(): pl.pallas_call(kernel, out_shape=(jax.ShapeDtypeStruct((COLS, OWN), f32),...]
where the time goes in v5:
time: 140 us
  Pallas kernels  139 us (99%)
    pallas_call x1, Pallas kernels, body(): pl.pallas_call(kernel, out_shape=(jax.ShapeDtypeStruct((COLS, OWN), f32),...  133 us
    pallas_call x1, Pallas kernels, body(): pl.pallas_call(store, out_shape=(jax.ShapeDtypeStruct((COLS, OWN), f32),...  6.44 us

profile of v5, /device:TPU:1, one launch (start us, length us, event | category | flops | bytes accessed | tf_op | source)
XLA Modules:
  0.0 140.0 jit_solution(6406681978233248085)
XLA Ops:
  0.6 133.0 %shard_map.76 = (f32[448,1024]{1,0:T(8,128)}, f32[448,1024]{1,0:T(8,128)}, bf16[448,4096]{1,0:T(8,128)(2,1)}) custom-call(s32[1,128]{1,0:T(1,128)} %seg_ref.1, bf16[128,4096]{1,0:T(8,128)(2,1)} %bitcast.15, bf16[448,4096]{1,0:T(8,128)(2,1)} %bitcast.9, f32[448,1024]{1,0:T(8,128)} %bitcast.11, f32[448,1024]{1,0:T(8,128)} %bitcast.12), custom_call_target="tpu_custom_call" | custom-call | flops 15032385536 | bytes 16777216 | tf_op jit(solution)/shard_map/pallas_call | solution.py:531
  133.6 6.4 %shard_map.77 = (f32[448,1024]{1,0:T(8,128)}, f32[448,1024]{1,0:T(8,128)}, bf16[448,4096]{1,0:T(8,128)(2,1)}) custom-call(f32[448,1024]{1,0:T(8,128)} %get-tuple-element.9.nb, f32[448,1024]{1,0:T(8,128)} %get-tuple-element.10.nm, bf16[448,4096]{1,0:T(8,128)(2,1)} %get-tuple-element.11.w), custom_call_target="tpu_custom_call" | custom-call | tf_op jit(solution)/shard_map/pallas_call | solution.py:570

commit v6 on v5

--- a/solution.py
+++ b/solution.py
@@ -22,7 +22,7 @@
 PASS = 1
 FWD = 3
 DIRECT = 1
-STORES = 4
+STORES = 2
 SHIP = UNITS - TILES + 2
 AHEAD = 3
 RELAYED = STEPS - 1
@@ -574,6 +574,7 @@
             jax.ShapeDtypeStruct((COLS, OWN), f32),
             jax.ShapeDtypeStruct((COLS, D), bf),
         ),
+        compiler_params=pltpu.CompilerParams(vmem_limit_bytes=60 * 2**20),
         grid=(STORES,),
         in_specs=[pl.BlockSpec((COLS // STORES, width), lambda i: (i, 0)) for width in (OWN, OWN, D)],
         out_specs=tuple(pl.BlockSpec((COLS // STORES, width), lambda i: (i, 0)) for width in (OWN, OWN, D)),

time: 140 us -> 139 us (level)
  no operation moved by 1% of the time
where the time goes in v6:
time: 139 us
  Pallas kernels  138 us (99%)
    pallas_call x1, Pallas kernels, body(): pl.pallas_call(kernel, out_shape=(jax.ShapeDtypeStruct((COLS, OWN), f32),...  133 us
    pallas_call x1, Pallas kernels, body(): pl.pallas_call(store, out_shape=(jax.ShapeDtypeStruct((COLS, OWN), f32),...  5.33 us

profile of v6, /device:TPU:1, one launch (start us, length us, event | category | flops | bytes accessed | tf_op | source)
XLA Modules:
  0.0 138.9 jit_solution(13575843748733700355)
XLA Ops:
  0.6 133.0 %shard_map.76 = (f32[448,1024]{1,0:T(8,128)}, f32[448,1024]{1,0:T(8,128)}, bf16[448,4096]{1,0:T(8,128)(2,1)}) custom-call(s32[1,128]{1,0:T(1,128)} %seg_ref.1, bf16[128,4096]{1,0:T(8,128)(2,1)} %bitcast.15, bf16[448,4096]{1,0:T(8,128)(2,1)} %bitcast.9, f32[448,1024]{1,0:T(8,128)} %bitcast.11, f32[448,1024]{1,0:T(8,128)} %bitcast.12), custom_call_target="tpu_custom_call" | custom-call | flops 15032385536 | bytes 16777216 | tf_op jit(solution)/shard_map/pallas_call | solution.py:531
  133.6 5.3 %shard_map.77 = (f32[448,1024]{1,0:T(8,128)}, f32[448,1024]{1,0:T(8,128)}, bf16[448,4096]{1,0:T(8,128)(2,1)}) custom-call(f32[448,1024]{1,0:T(8,128)} %get-tuple-element.9.nb, f32[448,1024]{1,0:T(8,128)} %get-tuple-element.10.nm, bf16[448,4096]{1,0:T(8,128)(2,1)} %get-tuple-element.11.w), custom_call_target="tpu_custom_call" | custom-call | tf_op jit(solution)/shard_map/pallas_call | solution.py:570

commit v7 on v6

--- a/solution.py
+++ b/solution.py
@@ -326,7 +326,7 @@
             cot[g, :, at] = (block * weight[i][None]).reshape(PART, TOK).astype(jnp.bfloat16)
             return carry
 
-        lax.fori_loop(0, TOK_G // TOK, tile, 0)
+        lax.fori_loop(0, TOK_G // TOK, tile, 0, unroll=4)
 
     def scale_own(u):
         @pl.when(at_home)

time: 139 us -> 139 us (level)
  no operation moved by 1% of the time
where the time goes in v7:
time: 139 us
  Pallas kernels  138 us (99%)
    pallas_call x1, Pallas kernels, body(): pl.pallas_call(kernel, out_shape=(jax.ShapeDtypeStruct((COLS, OWN), f32),...  133 us
    pallas_call x1, Pallas kernels, body(): pl.pallas_call(store, out_shape=(jax.ShapeDtypeStruct((COLS, OWN), f32),...  5.33 us

profile of v7, /device:TPU:1, one launch (start us, length us, event | category | flops | bytes accessed | tf_op | source)
XLA Modules:
  0.0 138.9 jit_solution(13929666496837395698)
XLA Ops:
  0.6 133.0 %shard_map.76 = (f32[448,1024]{1,0:T(8,128)}, f32[448,1024]{1,0:T(8,128)}, bf16[448,4096]{1,0:T(8,128)(2,1)}) custom-call(s32[1,128]{1,0:T(1,128)} %seg_ref.1, bf16[128,4096]{1,0:T(8,128)(2,1)} %bitcast.15, bf16[448,4096]{1,0:T(8,128)(2,1)} %bitcast.9, f32[448,1024]{1,0:T(8,128)} %bitcast.11, f32[448,1024]{1,0:T(8,128)} %bitcast.12), custom_call_target="tpu_custom_call" | custom-call | flops 15032385536 | bytes 16777216 | tf_op jit(solution)/shard_map/pallas_call | solution.py:531
  133.6 5.3 %shard_map.77 = (f32[448,1024]{1,0:T(8,128)}, f32[448,1024]{1,0:T(8,128)}, bf16[448,4096]{1,0:T(8,128)(2,1)}) custom-call(f32[448,1024]{1,0:T(8,128)} %get-tuple-element.9.nb, f32[448,1024]{1,0:T(8,128)} %get-tuple-element.10.nm, bf16[448,4096]{1,0:T(8,128)(2,1)} %get-tuple-element.11.w), custom_call_target="tpu_custom_call" | custom-call | tf_op jit(solution)/shard_map/pallas_call | solution.py:570
